TPU v7x, 32 devices: a whole 2x2x4 slice. The times are simulated.
32 devices in a mesh: dp: 8 (over y, x, core), fsdp: 4 (over z).
Axes of the slice: x: 2, y: 2, z: 4, core: 2. Of those that a mesh axis runs over, the one named last changes fastest.
Arguments:
- tokens: bfloat16 [8192, 2048], P(('dp', 'fsdp')), may hold values from -6 to 6
- text: bfloat16 [32, 128, 2048], P(('dp', 'fsdp')), may hold values from -6 to 6
- cotangent: bfloat16 [32, 128, 2048], P(('dp', 'fsdp')), may hold values from -6 to 6
- positions: int32 [32, 128], P(('dp', 'fsdp')), may hold values from 0 to 255, as said below
- text_lengths: int32 [32], P(('dp', 'fsdp')), may hold values from 1 to 128, as said below
- mask_embed: bfloat16 [2048], P(('dp', 'fsdp')), may hold values from -6 to 6
- gain_attn: bfloat16 [2048], P(('dp', 'fsdp')), may hold values from 0.099609375 to 1.8984375
- w_qkv: bfloat16 [2048, 6144], P(('dp', 'fsdp')), may hold values from -0.125 to 0.125
- w_attn_out: bfloat16 [2048, 2048], P(('dp', 'fsdp')), may hold values from -1 to 1
- gain_cross: bfloat16 [2048], P(('dp', 'fsdp')), may hold values from 0.099609375 to 1.8984375
- w_cross_q: bfloat16 [2048, 2048], P(('dp', 'fsdp')), may hold values from -0.125 to 0.125
- w_cross_kv: bfloat16 [2048, 4096], P(('dp', 'fsdp')), may hold values from -0.125 to 0.125
- w_cross_out: bfloat16 [2048, 2048], P(('dp', 'fsdp')), may hold values from -0.75 to 0.75
- gain_mlp: bfloat16 [2048], P(('dp', 'fsdp')), may hold values from 0.099609375 to 1.8984375
- w_up: bfloat16 [2048, 8192], P(('dp', 'fsdp')), may hold values from -0.125 to 0.125
- w_down: bfloat16 [8192, 2048], P(('dp', 'fsdp')), may hold values from -0.0625 to 0.0625
Outputs:
- output: bfloat16 [8192, 2048], P(('dp', 'fsdp'))
- grad_tokens: bfloat16 [8192, 2048], P(('dp', 'fsdp'))
- grad_text: bfloat16 [32, 128, 2048], P(('dp', 'fsdp'))
- grad_mask_embed: float32 [2048], P(('dp', 'fsdp'))
- grad_gain_attn: float32 [2048], P(('dp', 'fsdp'))
- grad_w_qkv: float32 [2048, 6144], P(('dp', 'fsdp'))
- grad_w_attn_out: float32 [2048, 2048], P(('dp', 'fsdp'))
- grad_gain_cross: float32 [2048], P(('dp', 'fsdp'))
- grad_w_cross_q: float32 [2048, 2048], P(('dp', 'fsdp'))
- grad_w_cross_kv: float32 [2048, 4096], P(('dp', 'fsdp'))
- grad_w_cross_out: float32 [2048, 2048], P(('dp', 'fsdp'))
- grad_gain_mlp: float32 [2048], P(('dp', 'fsdp'))
- grad_w_up: float32 [2048, 8192], P(('dp', 'fsdp'))
- grad_w_down: float32 [8192, 2048], P(('dp', 'fsdp'))
Inputs may be any that keep to these rules, and one draw needn't show every extreme that they name: Each image's row holds 128 distinct positions. `text_lengths`: some image has all 128 text tokens valid.
All inputs are finite; a program needn't handle non-finite values.
Results may differ from a plain program's by a relative error of at most 0.02.
Values may be sent and summed in bfloat16 or wider, within the bound.
No kernel may reach another device: no remote copies, remote signals or barrier semaphores. Data moves between devices by JAX's collectives and lax.ppermute only.
A program may use at most 576 MiB of HBM per device.

v0:
```python
import jax
import jax.numpy as jnp
from jax import lax
from jax.sharding import PartitionSpec as P

HEADS = 16
HDIM = 128


def as_sent(shard):
    return jax.tree.map(lambda a: a.astype(jnp.bfloat16) if a.dtype == jnp.float32 else a, shard)


def normed(stream):
    centered = stream - jnp.mean(stream, axis=-1, keepdims=True)
    return centered * lax.rsqrt(jnp.mean(centered * centered, axis=-1, keepdims=True) + 1e-05)


def heads_of(block, images):
    return block.reshape(images, -1, HEADS, HDIM)


def scores_of(queries, key_heads, text_valid):
    logits = jnp.einsum(
        "bqhe,bkhe->bhqk", queries, key_heads, preferred_element_type=jnp.float32
    ) * HDIM ** (-0.5)
    if text_valid is not None:
        logits = jnp.where(text_valid[:, None, None, :], logits, -1e30)
    return jax.nn.softmax(logits, axis=-1)


def mix_rows(softmaxed, value_heads, rows_shape):
    low_probs = softmaxed.astype(jnp.bfloat16)
    mixture = jnp.einsum(
        "bhqk,bkhe->bqhe", low_probs, value_heads, preferred_element_type=jnp.float32
    )
    return (low_probs, mixture.reshape(rows_shape).astype(jnp.bfloat16))


def attend_back(queries, key_heads, value_heads, softmaxed, low_probs, grad_mix):
    grad_probs = jnp.einsum(
        "bqhe,bkhe->bhqk", grad_mix, value_heads, preferred_element_type=jnp.float32
    )
    grad_values = jnp.einsum(
        "bhqk,bqhe->bkhe", low_probs, grad_mix, preferred_element_type=jnp.float32
    )
    grad_logits = softmaxed * (grad_probs - jnp.sum(grad_probs * softmaxed, axis=-1, keepdims=True))
    grad_logits = grad_logits.astype(jnp.bfloat16)
    grad_query = jnp.einsum(
        "bhqk,bkhe->bqhe", grad_logits, key_heads, preferred_element_type=jnp.float32
    ) * HDIM ** (-0.5)
    grad_keys = jnp.einsum(
        "bhqk,bqhe->bkhe", grad_logits, queries, preferred_element_type=jnp.float32
    ) * HDIM ** (-0.5)
    return (grad_query, grad_keys, grad_values)


def fetch_forward(weights):
    return jax.tree.map(
        lambda part, own: part.astype(own.dtype),
        lax.all_gather(as_sent(weights), ("dp", "fsdp"), axis=0, tiled=True),
        weights,
    )


def fetch_backward(weights):
    return jax.tree.map(
        lambda part, own: part.astype(own.dtype),
        lax.all_gather(as_sent(weights), ("dp", "fsdp"), axis=0, tiled=True),
        weights,
    )


def reduce_grads(gradients):
    return lax.psum_scatter(gradients, ("dp", "fsdp"), scatter_dimension=0, tiled=True)


def self_inner(stream, attn_set, images):
    gain_vec, w_packed, w_out = attn_set
    model_width = stream.shape[1]
    norm_field, norm_back = jax.vjp(normed, stream)
    entries = (norm_field * gain_vec.astype(jnp.float32)).astype(jnp.bfloat16)
    packed = jnp.dot(entries, w_packed, preferred_element_type=jnp.float32).astype(jnp.bfloat16)
    queries = heads_of(packed[:, :model_width], images)
    key_heads = heads_of(packed[:, model_width : 2 * model_width], images)
    value_heads = heads_of(packed[:, 2 * model_width :], images)
    softmaxed = scores_of(queries, key_heads, None)
    return (norm_field, norm_back, entries, queries, key_heads, value_heads, softmaxed)


def self_out(stream, attn_set, images):
    norm_field, norm_back, entries, queries, key_heads, value_heads, softmaxed = self_inner(
        stream, attn_set, images
    )
    low_probs, mixture = mix_rows(softmaxed, value_heads, stream.shape)
    return jnp.dot(mixture, attn_set[2], preferred_element_type=jnp.float32)


def self_back(stream, gradient, attn_set, images):
    norm_field, norm_back, entries, queries, key_heads, value_heads, softmaxed = self_inner(
        stream, attn_set, images
    )
    low_probs, mixture = mix_rows(softmaxed, value_heads, stream.shape)
    grad_low = gradient.astype(jnp.bfloat16)
    grad_out_w = jnp.dot(mixture.T, grad_low, preferred_element_type=jnp.float32)
    grad_mix = heads_of(
        jnp.dot(grad_low, attn_set[2].T, preferred_element_type=jnp.float32).astype(jnp.bfloat16),
        images,
    )
    grad_query, grad_keys, grad_values = attend_back(
        queries, key_heads, value_heads, softmaxed, low_probs, grad_mix
    )
    grad_packed = jnp.concatenate(
        [
            grad_query.reshape(stream.shape),
            grad_keys.reshape(stream.shape),
            grad_values.reshape(stream.shape),
        ],
        axis=1,
    ).astype(jnp.bfloat16)
    grad_packed_w = jnp.dot(entries.T, grad_packed, preferred_element_type=jnp.float32)
    grad_entries = jnp.dot(grad_packed, attn_set[1].T, preferred_element_type=jnp.float32)
    grad_gain = jnp.sum(grad_entries * norm_field, axis=0)
    gradient = gradient + norm_back(grad_entries * attn_set[0].astype(jnp.float32))[0]
    return (gradient, (grad_gain, grad_packed_w, grad_out_w))


def cross_inner(stream, text_rows, text_valid, cross_set, images):
    gain_vec, w_query, w_pair, w_out = cross_set
    model_width = stream.shape[1]
    norm_field, norm_back = jax.vjp(normed, stream)
    entries = (norm_field * gain_vec.astype(jnp.float32)).astype(jnp.bfloat16)
    queries = heads_of(
        jnp.dot(entries, w_query, preferred_element_type=jnp.float32).astype(jnp.bfloat16), images
    )
    text_pair = jnp.dot(text_rows, w_pair, preferred_element_type=jnp.float32).astype(jnp.bfloat16)
    key_heads = heads_of(text_pair[:, :model_width], images)
    value_heads = heads_of(text_pair[:, model_width:], images)
    softmaxed = scores_of(queries, key_heads, text_valid)
    return (norm_field, norm_back, entries, queries, key_heads, value_heads, softmaxed)


def cross_out(stream, text_rows, text_valid, cross_set, images):
    norm_field, norm_back, entries, queries, key_heads, value_heads, softmaxed = cross_inner(
        stream, text_rows, text_valid, cross_set, images
    )
    low_probs, mixture = mix_rows(softmaxed, value_heads, stream.shape)
    return jnp.dot(mixture, cross_set[3], preferred_element_type=jnp.float32)


def cross_back(stream, text_rows, text_valid, gradient, cross_set, images):
    norm_field, norm_back, entries, queries, key_heads, value_heads, softmaxed = cross_inner(
        stream, text_rows, text_valid, cross_set, images
    )
    low_probs, mixture = mix_rows(softmaxed, value_heads, stream.shape)
    grad_low = gradient.astype(jnp.bfloat16)
    grad_out_w = jnp.dot(mixture.T, grad_low, preferred_element_type=jnp.float32)
    grad_mix = heads_of(
        jnp.dot(grad_low, cross_set[3].T, preferred_element_type=jnp.float32).astype(jnp.bfloat16),
        images,
    )
    grad_query, grad_keys, grad_values = attend_back(
        queries, key_heads, value_heads, softmaxed, low_probs, grad_mix
    )
    grad_query = grad_query.reshape(stream.shape).astype(jnp.bfloat16)
    grad_pair = jnp.concatenate(
        [grad_keys.reshape(text_rows.shape), grad_values.reshape(text_rows.shape)], axis=1
    ).astype(jnp.bfloat16)
    grad_pair_w = jnp.dot(text_rows.T, grad_pair, preferred_element_type=jnp.float32)
    grad_text = jnp.dot(grad_pair, cross_set[2].T, preferred_element_type=jnp.float32).astype(
        jnp.bfloat16
    )
    grad_query_w = jnp.dot(entries.T, grad_query, preferred_element_type=jnp.float32)
    grad_entries = jnp.dot(grad_query, cross_set[1].T, preferred_element_type=jnp.float32)
    grad_gain = jnp.sum(grad_entries * norm_field, axis=0)
    gradient = gradient + norm_back(grad_entries * cross_set[0].astype(jnp.float32))[0]
    return (gradient, (grad_gain, grad_query_w, grad_pair_w, grad_out_w), grad_text)


def mlp_inner(stream, mlp_set):
    norm_field, norm_back = jax.vjp(normed, stream)
    entries = (norm_field * mlp_set[0].astype(jnp.float32)).astype(jnp.bfloat16)
    hidden_pre = jnp.dot(entries, mlp_set[1], preferred_element_type=jnp.float32)
    active = jax.nn.gelu(hidden_pre).astype(jnp.bfloat16)
    return (norm_field, norm_back, entries, hidden_pre, active)


def mlp_out(stream, mlp_set):
    norm_field, norm_back, entries, hidden_pre, active = mlp_inner(stream, mlp_set)
    return jnp.dot(active, mlp_set[2], preferred_element_type=jnp.float32)


def mlp_back(stream, gradient, mlp_set):
    norm_field, norm_back, entries, hidden_pre, active = mlp_inner(stream, mlp_set)
    grad_low = gradient.astype(jnp.bfloat16)
    grad_down_w = jnp.dot(active.T, grad_low, preferred_element_type=jnp.float32)
    grad_active = jnp.dot(grad_low, mlp_set[2].T, preferred_element_type=jnp.float32)
    unused_value, gelu_back = jax.vjp(jax.nn.gelu, hidden_pre)
    grad_pre = gelu_back(grad_active)[0].astype(jnp.bfloat16)
    grad_up_w = jnp.dot(entries.T, grad_pre, preferred_element_type=jnp.float32)
    grad_entries = jnp.dot(grad_pre, mlp_set[1].T, preferred_element_type=jnp.float32)
    grad_gain = jnp.sum(grad_entries * norm_field, axis=0)
    gradient = gradient + norm_back(grad_entries * mlp_set[0].astype(jnp.float32))[0]
    return (gradient, (grad_gain, grad_up_w, grad_down_w))


def shards(
    tokens,
    text,
    cotangent,
    positions,
    text_lengths,
    mask_embed,
    gain_attn,
    w_qkv,
    w_attn_out,
    gain_cross,
    w_cross_q,
    w_cross_kv,
    w_cross_out,
    gain_mlp,
    w_up,
    w_down,
):
    images = cotangent.shape[0]
    model_width = cotangent.shape[2]
    seq_len = tokens.shape[0] // images
    select = (positions[:, :, None] == lax.broadcasted_iota(jnp.int32, (1, 1, seq_len), 2)).astype(
        jnp.float32
    )
    masked = jnp.sum(select, axis=1).reshape(-1, 1)
    text_valid = lax.broadcasted_iota(jnp.int32, (1, text.shape[1]), 1) < text_lengths[:, None]
    text_rows = text.reshape(-1, model_width)
    attn_set = fetch_forward((mask_embed, gain_attn, w_qkv, w_attn_out))
    start_rows = (
        tokens.astype(jnp.float32) * (1.0 - masked)
        + masked * attn_set[0].astype(jnp.float32)[None, :]
    )
    after_attn = start_rows + self_out(start_rows, attn_set[1:], images)
    cross_set = fetch_forward((gain_cross, w_cross_q, w_cross_kv, w_cross_out))
    after_cross = after_attn + cross_out(after_attn, text_rows, text_valid, cross_set, images)
    mlp_set = fetch_forward((gain_mlp, w_up, w_down))
    output = (after_cross + mlp_out(after_cross, mlp_set)).astype(jnp.bfloat16)
    gradient = jnp.einsum(
        "bms,bmd->bsd", select.astype(jnp.bfloat16), cotangent, preferred_element_type=jnp.float32
    ).reshape(-1, model_width)
    mlp_set = fetch_backward((gain_mlp, w_up, w_down))
    gradient, mlp_grads = mlp_back(after_cross, gradient, mlp_set)
    mlp_grads = reduce_grads(mlp_grads)
    cross_set = fetch_backward((gain_cross, w_cross_q, w_cross_kv, w_cross_out))
    gradient, cross_grads, grad_text = cross_back(
        after_attn, text_rows, text_valid, gradient, cross_set, images
    )
    cross_grads = reduce_grads(cross_grads)
    attn_set = fetch_backward((gain_attn, w_qkv, w_attn_out))
    gradient, attn_grads = self_back(start_rows, gradient, attn_set, images)
    grad_embed = jnp.sum(gradient * masked, axis=0)
    attn_grads = reduce_grads((grad_embed, attn_grads[0], attn_grads[1], attn_grads[2]))
    grad_tokens = (gradient * (1.0 - masked)).astype(jnp.bfloat16)
    return (
        output,
        grad_tokens,
        grad_text.reshape(text.shape),
        attn_grads[0],
        attn_grads[1],
        attn_grads[2],
        attn_grads[3],
        cross_grads[0],
        cross_grads[1],
        cross_grads[2],
        cross_grads[3],
        mlp_grads[0],
        mlp_grads[1],
        mlp_grads[2],
    )


def solution(mesh):
    placed = (
        P(("dp", "fsdp"), None),
        P(("dp", "fsdp"), None, None),
        P(("dp", "fsdp"), None, None),
        P(("dp", "fsdp"), None),
        P(("dp", "fsdp")),
        P(("dp", "fsdp")),
        P(("dp", "fsdp")),
        P(("dp", "fsdp"), None),
        P(("dp", "fsdp"), None),
        P(("dp", "fsdp")),
        P(("dp", "fsdp"), None),
        P(("dp", "fsdp"), None),
        P(("dp", "fsdp"), None),
        P(("dp", "fsdp")),
        P(("dp", "fsdp"), None),
        P(("dp", "fsdp"), None),
    )
    return jax.shard_map(
        shards,
        mesh=mesh,
        in_specs=placed,
        out_specs=(
            P(("dp", "fsdp"), None),
            P(("dp", "fsdp"), None),
            P(("dp", "fsdp"), None, None),
            P(("dp", "fsdp")),
            P(("dp", "fsdp")),
            P(("dp", "fsdp"), None),
            P(("dp", "fsdp"), None),
            P(("dp", "fsdp")),
            P(("dp", "fsdp"), None),
            P(("dp", "fsdp"), None),
            P(("dp", "fsdp"), None),
            P(("dp", "fsdp")),
            P(("dp", "fsdp"), None),
            P(("dp", "fsdp"), None),
        ),
        check_vma=False,
    )
```

profile of v0, /device:TPU:0, one launch (start us, length us, event | category | flops | bytes accessed | tf_op | source)
XLA Modules:
  0.0 6066.8 jit_solution(18066372382172671311)
XLA Ops:
  13.1 43.1 all-reduce.9
  58.1 1.9 fusion.35
  60.0 69.5 %all-gather.12.cloned.1.call-done = bf16[2048,4096]{1,0:T(8,128)(2,1)} async-done(((bf16[64,4096]{1,0:T(8,128)(2,1)}), bf16[2048,4096]{1,0:T(8,128)(2,1)}) %all-gather.12.cloned.1.call-update) | async-done | bytes 16777232 | tf_op jit(solution)/shard_map/all_gather | solution.py:61
  129.5 8.1 convolution_convert_fusion.1
  138.8 146.5 %all-gather.8.cloned.1.call-done = bf16[2048,6144]{1,0:T(8,128)(2,1)} async-done(((bf16[64,6144]{1,0:T(8,128)(2,1)}), bf16[2048,6144]{1,0:T(8,128)(2,1)}) %all-gather.8.cloned.1.call-update) | async-done | bytes 25165840 | tf_op jit(solution)/shard_map/all_gather | solution.py:61
  285.3 12.0 convolution_convert_fusion
  297.3 1.5 fusion.78
  299.4 2.3 copy.141
  301.7 3.5 fusion.80
  305.2 4.1 convolution_convert_fusion.7
  309.3 54.5 all-gather.10.cloned.1.call-done
  363.8 6.5 fusion.81
  370.7 71.9 %all-gather.14.cloned.1.call-done = bf16[2048,2048]{1,0:T(8,128)(2,1)} async-done(((bf16[64,2048]{1,0:T(8,128)(2,1)}), bf16[2048,2048]{1,0:T(8,128)(2,1)}) %all-gather.14.cloned.1.call-update) | async-done | bytes 8388624 | tf_op jit(solution)/shard_map/all_gather | solution.py:61
  442.6 6.7 convolution_convert_fusion.4
  449.3 2.2 copy.142
  451.6 3.5 fusion.82
  455.1 3.2 convolution_convert_fusion.8
  458.3 63.1 %all-gather.16.cloned.1.call-done = bf16[2048,2048]{1,0:T(8,128)(2,1)} async-done(((bf16[64,2048]{1,0:T(8,128)(2,1)}), bf16[2048,2048]{1,0:T(8,128)(2,1)}) %all-gather.16.cloned.1.call-update) | async-done | bytes 8388624 | tf_op jit(solution)/shard_map/all_gather | solution.py:61
  521.4 6.1 fusion.83
  527.6 1.3 copy-done.2
  529.2 188.4 %all-gather.18.cloned.1.call-done = bf16[2048,8192]{1,0:T(8,128)(2,1)} async-done(((bf16[64,8192]{1,0:T(8,128)(2,1)}), bf16[2048,8192]{1,0:T(8,128)(2,1)}) %all-gather.18.cloned.1.call-update) | async-done | bytes 33554448 | tf_op jit(solution)/shard_map/all_gather | solution.py:61
  717.6 18.9 fusion.74
  736.5 177.0 %all-gather.20.cloned.1.call-done = bf16[8192,2048]{1,0:T(8,128)(2,1)} async-done(((bf16[256,2048]{1,0:T(8,128)(2,1)}), bf16[8192,2048]{1,0:T(8,128)(2,1)}) %all-gather.20.cloned.1.call-update) | async-done | bytes 33554448 | tf_op jit(solution)/shard_map/all_gather | solution.py:61
  913.5 21.1 fusion.8
  934.7 18.8 multiply_reduce_fusion.2
  953.4 3.0 fusion.77
  956.7 1.4 copy-done.8
  958.1 6.7 convolution_convert_fusion.3
  964.8 2.3 copy.144
  967.1 2.6 multiply_reduce_fusion.8
  970.3 0.9 copy-done.14
  971.7 7.2 multiply_reduce_fusion.3
  979.5 0.9 copy-done.9
  980.8 1.4 copy-done.11
  982.1 8.1 fusion.39
  990.5 9.5 fusion.72
  1000.0 1.5 copy-done.10
  1001.5 9.3 fusion.42
  1010.9 1.5 copy-done.12
  1012.5 6.8 convolution_convert_fusion.2
  1019.2 1.6 copy.145
  1020.8 3.1 multiply_reduce_fusion
  1029.2 20.2 fusion.20
  1049.7 0.9 copy-done.15
  1051.4 1.2 copy-done.29
  1052.6 1.7 convolution_convert_fusion.9
  1055.1 14.5 convolution_bitcast_fusion
  1069.6 31.3 copy.138
  1100.9 1.5 copy-done.3
  1102.4 25.8 fusion.73
  1128.7 28.2 fusion.45
  1157.0 14.5 multiply_reduce_fusion.4
  1171.5 2.7 fusion.75
  1174.3 1.5 multiply_reduce_fusion.5
  1175.8 43.3 all-reduce.8
  1221.4 12.4 fusion.13
  1233.8 19.7 fusion.12
  1253.5 100.1 %reduce-scatter.12.cloned.1.call-done = f32[64,2048]{1,0:T(8,128)} async-done(((f32[2048,2048]{1,0:T(8,128)}), f32[64,2048]{1,0:T(8,128)}) %reduce-scatter.12.cloned.1.call-update) | async-done | bytes 524304 | tf_op jit(solution)/shard_map/reduce_scatter | solution.py:75
  1353.6 365.1 %reduce-scatter.14.cloned.1.call-done = f32[64,2048]{1,0:T(8,128)} async-done(((f32[2048,2048]{1,0:T(8,128)}), f32[64,2048]{1,0:T(8,128)}) %reduce-scatter.14.cloned.1.call-update) | async-done | bytes 524304 | tf_op jit(solution)/shard_map/reduce_scatter | solution.py:75
  1718.7 364.9 %reduce-scatter.16.cloned.1.call-done = f32[64,2048]{1,0:T(8,128)} async-done(((f32[2048,2048]{1,0:T(8,128)}), f32[64,2048]{1,0:T(8,128)}) %reduce-scatter.16.cloned.1.call-update) | async-done | bytes 524304 | tf_op jit(solution)/shard_map/reduce_scatter | solution.py:75
  2083.6 436.4 %reduce-scatter.10.cloned.1.call-done = f32[64,6144]{1,0:T(8,128)} async-done(((f32[2048,6144]{1,0:T(8,128)}), f32[64,6144]{1,0:T(8,128)}) %reduce-scatter.10.cloned.1.call-update) | async-done | bytes 1572880 | tf_op jit(solution)/shard_map/reduce_scatter | solution.py:75
  2520.0 713.7 %reduce-scatter.22.cloned.1.call-done = f32[64,4096]{1,0:T(8,128)} async-done(((f32[2048,4096]{1,0:T(8,128)}), f32[64,4096]{1,0:T(8,128)}) %reduce-scatter.22.cloned.1.call-update) | async-done | bytes 1048592
  3233.7 1412.9 %reduce-scatter.18.cloned.1.call-done = f32[64,8192]{1,0:T(8,128)} async-done(((f32[2048,8192]{1,0:T(8,128)}), f32[64,8192]{1,0:T(8,128)}) %reduce-scatter.18.cloned.1.call-update) | async-done | bytes 2097168 | tf_op jit(solution)/shard_map/reduce_scatter | solution.py:75
  4646.6 1413.5 %reduce-scatter.20.cloned.1.call-done = f32[256,2048]{1,0:T(8,128)} async-done(((f32[8192,2048]{1,0:T(8,128)}), f32[256,2048]{1,0:T(8,128)}) %reduce-scatter.20.cloned.1.call-update) | async-done | bytes 2097168 | tf_op jit(solution)/shard_map/reduce_scatter | solution.py:75
  (174 shorter events, 21.7 us)
Async XLA Ops:
  7.2 122.3 %copy-start = (bf16[1,128,2048]{2,1,0:T(8,128)(2,1)S(1)}, bf16[1,128,2048]{2,1,0:T(8,128)(2,1)}, u32[]{:S(2)}) copy-start(bf16[1,128,2048]{2,1,0:T(8,128)(2,1)} %param.17) | copy-start | bytes 1572868
  7.2 4.8 copy-start.50
  7.2 5.1 copy-start.51
  7.2 5.3 copy-start.52
  7.2 5.6 copy-start.53
  7.2 49.6 copy-start.49
  7.2 49.7 copy-start.4
  7.3 122.3 %all-gather.12.cloned.1.call-start = ((), (), s32[]{:S(2)}) async-start(), calls=%async_computation.9 | async-start | bytes 17301504 | tf_op jit(solution)/shard_map/all_gather | solution.py:61
  8.0 277.3 %all-gather.8.cloned.1.call-start = ((), (), s32[]{:S(2)}) async-start(), calls=%async_computation.7 | async-start | bytes 25952256 | tf_op jit(solution)/shard_map/all_gather | solution.py:61
  8.7 355.1 %all-gather.10.cloned.1.call-start = ((), (), s32[]{:S(2)}) async-start(), calls=%async_computation.8 | async-start | bytes 8650752 | tf_op jit(solution)/shard_map/all_gather | solution.py:61
  9.5 433.1 %all-gather.14.cloned.1.call-start = ((), (), s32[]{:S(2)}) async-start(), calls=%async_computation.10 | async-start | bytes 8650752 | tf_op jit(solution)/shard_map/all_gather | solution.py:61
  10.1 511.3 %all-gather.16.cloned.1.call-start = ((), (), s32[]{:S(2)}) async-start(), calls=%async_computation.11 | async-start | bytes 8650752 | tf_op jit(solution)/shard_map/all_gather | solution.py:61
  10.6 47.5 copy-start.36
  10.7 706.9 %all-gather.18.cloned.1.call-start = ((), (), s32[]{:S(2)}) async-start(), calls=%async_computation.12 | async-start | bytes 34603008 | tf_op jit(solution)/shard_map/all_gather | solution.py:61
  11.2 902.3 %all-gather.20.cloned.1.call-start = ((), (), s32[]{:S(2)}) async-start(), calls=%async_computation.13 | async-start | bytes 34603008 | tf_op jit(solution)/shard_map/all_gather | solution.py:61
  12.0 1341.7 %reduce-scatter.12.cloned.1.call-start = ((), (), s32[]{:S(2)}) async-start(), calls=%async_computation.15 | async-start | bytes 17301504 | tf_op jit(solution)/shard_map/reduce_scatter | solution.py:75
  56.1 229.2 %copy-start.34 = (f32[2048]{0:T(1024)}, f32[2048]{0:T(1024)S(1)}, u32[]{:S(2)}) copy-start(f32[2048]{0:T(1024)S(1)} %convert_element_type.186) | copy-start | bytes 24580
  56.1 307.7 %copy-start.30 = (f32[2048]{0:T(1024)}, f32[2048]{0:T(1024)S(1)}, u32[]{:S(2)}) copy-start(f32[2048]{0:T(1024)S(1)} %convert_element_type.185) | copy-start | bytes 24580
  56.9 306.9 %copy-start.37 = (f32[256]{0:T(256)}, f32[256]{0:T(256)S(1)}, u32[]{:S(2)}) copy-start(f32[256]{0:T(256)S(1)} %convert_reduce_fusion) | copy-start | bytes 3076
  57.0 306.9 %copy-start.39 = (f32[256]{0:T(256)}, f32[256]{0:T(256)S(1)}, u32[]{:S(2)}) copy-start(f32[256]{0:T(256)S(1)} %broadcast_subtract_fusion) | copy-start | bytes 3076
  57.5 227.8 %copy-start.41 = (f32[256]{0:T(256)}, f32[256]{0:T(256)S(1)}, u32[]{:S(2)}) copy-start(f32[256]{0:T(256)S(1)} %broadcast_multiply_fusion.2) | copy-start | bytes 3076
  58.1 79.5 %copy-start.45 = (f32[256]{0:T(256)}, f32[256]{0:T(256)S(1)}, u32[]{:S(2)}) copy-start(f32[256]{0:T(256)S(1)} %multiply_reduce_fusion.12) | copy-start | bytes 3076
  58.1 227.1 %copy-start.43 = (f32[256]{0:T(256)}, f32[256]{0:T(256)S(1)}, u32[]{:S(2)}) copy-start(f32[256]{0:T(256)S(1)} %fusion.62) | copy-start | bytes 3076
  299.4 5.8 copy-start.21
  301.7 3.5 copy-start.23
  527.5 1.3 copy-start.2
  953.4 3.0 copy-start.7
  956.7 1.4 copy-start.8
  967.1 2.7 copy-start.28
  971.7 7.2 copy-start.25
  978.9 1.6 copy-start.9
  980.5 1.7 copy-start.16
  980.8 1.4 copy-start.11
  990.2 728.4 %reduce-scatter.14.cloned.1.call-start = ((), (), s32[]{:S(2)}) async-start(), calls=%async_computation.16 | async-start | bytes 17301504 | tf_op jit(solution)/shard_map/reduce_scatter | solution.py:75
  999.9 1.6 copy-start.10
  1000.0 1083.6 %reduce-scatter.16.cloned.1.call-start = ((), (), s32[]{:S(2)}) async-start(), calls=%async_computation.17 | async-start | bytes 17301504 | tf_op jit(solution)/shard_map/reduce_scatter | solution.py:75
  1010.8 1.6 copy-start.12
  1010.9 1509.2 %reduce-scatter.10.cloned.1.call-start = ((), (), s32[]{:S(2)}) async-start(), calls=%async_computation.14 | async-start | bytes 51904512 | tf_op jit(solution)/shard_map/reduce_scatter | solution.py:75
  1019.2 1.6 copy-start.33
  1020.8 3.5 copy-start.17
  1024.3 1.2 copy-start.22
  1025.6 1.2 copy-start.24
  1026.8 1.4 copy-start.19
  1027.3 1.9 copy-start.5
  1027.3 1.9 copy-start.31
  1027.3 1.9 copy-start.35
  1027.3 1.9 copy-start.38
  1027.3 1.9 copy-start.40
  1027.3 1.9 copy-start.42
  1027.3 1.9 copy-start.44
  1049.4 1.2 copy-start.15
  1049.4 1.5 copy-start.18
  1049.5 2184.2 %reduce-scatter.22.cloned.1.call-start = ((), (), s32[]{:S(2)}) async-start(), calls=%async_computation.20 | async-start | bytes 34603008
  1051.0 1.6 copy-start.29
  1100.8 1.6 copy-start.3
  1100.9 3545.7 %reduce-scatter.18.cloned.1.call-start = ((), (), s32[]{:S(2)}) async-start(), calls=%async_computation.18 | async-start | bytes 69206016 | tf_op jit(solution)/shard_map/reduce_scatter | solution.py:75
  1128.3 4931.8 %reduce-scatter.20.cloned.1.call-start = ((), (), s32[]{:S(2)}) async-start(), calls=%async_computation.19 | async-start | bytes 69206016 | tf_op jit(solution)/shard_map/reduce_scatter | solution.py:75
  1157.0 14.5 copy-start.46
  1157.0 14.5 copy-start.6
  1171.5 2.7 copy-start.13
  1174.2 1.5 copy-start.47
  1174.2 1.5 copy-start.48
  1174.2 47.2 copy-start.27
  1233.8 4826.3 %copy-start.1 = (bf16[1,128,2048]{2,1,0:T(8,128)(2,1)S(1)}, bf16[1,128,2048]{2,1,0:T(8,128)(2,1)}, u32[]{:S(2)}) copy-start(bf16[1,128,2048]{2,1,0:T(8,128)(2,1)} %param.17) | copy-start | bytes 1572868
  (4 other events, 3.7 us)
Sparse Core Ops, SparseCore 0:
  11.1 118.3 all-gather.11
  132.4 152.8 all-gather.7
  288.2 75.5 all-gather.9
  366.6 75.9 all-gather.13
  445.4 75.9 all-gather.15
  524.2 193.3 all-gather.17
  720.5 192.9 all-gather.19
  990.4 363.2 reduce-scatter.11
  1356.5 362.1 reduce-scatter.13
  1721.4 362.1 reduce-scatter.15
  2090.6 429.3 reduce-scatter.9
  2522.7 710.8 reduce-scatter.21
  3236.6 1409.9 reduce-scatter.17
  4649.4 1410.6 reduce-scatter.19
where the time goes:
time: 6080 us; the launch traced here: 6070 us
  waiting for transfers between devices  5580 us (92%)
  matrix products  308 us (5%)
  blocking collectives  86.4 us (1%)
  local copies, waits for them, and re-layouts  62.3 us (1%)
    reduce_scatter x6, waiting for transfers between devices, reduce_grads(): lax.psum_scatter(gradients, ('dp', 'fsdp'), scatter_dimension=0, tiled=True)  4090 us
    all_gather x7, waiting for transfers between devices, fetch_forward(): lax.all_gather(as_sent(weights), ('dp', 'fsdp'), axis=0, tiled=True)  771 us
    unnamed x15, waiting for transfers between devices  718 us
  transfers between devices with their start and end apart: 14, of which 14 were waited for; matrix products, arithmetic and copies ran while one was open for 5% of the time, Pallas kernels for 0%

commit v1 on v0

v1 whole, which is shorter than its diff:
```python
import jax
import jax.numpy as jnp
from jax import lax
from jax.sharding import Mesh, PartitionSpec as P

HEADS = 16
HDIM = 128
PAD = 16
BF = jnp.bfloat16
F32 = jnp.float32


def dot(left, right):
    return jnp.dot(left, right, preferred_element_type=F32)


def dot_t(left, right):
    return lax.dot_general(left, right, (((1,), (1,)), ((), ())), preferred_element_type=F32)


def dot_sum(left, right):
    return lax.dot_general(left, right, (((0,), (0,)), ((), ())), preferred_element_type=F32)


def normed(rows):
    centered = rows - jnp.mean(rows, axis=-1, keepdims=True)
    scale = lax.rsqrt(jnp.mean(centered * centered, axis=-1, keepdims=True) + 1e-05)
    return centered * scale, scale


def norm_back(grad, field, scale):
    return scale * (
        grad
        - jnp.mean(grad, axis=-1, keepdims=True)
        - field * jnp.mean(grad * field, axis=-1, keepdims=True)
    )


def xor_order(stack, me, size):
    bit = 1
    while bit < size:
        split = stack.reshape((size // (2 * bit), 2, bit) + stack.shape[1:])
        stack = jnp.where((me & bit) != 0, split[:, ::-1], split).reshape(stack.shape)
        bit *= 2
    return stack


def bits_of(size):
    return [1 << k for k in range(size.bit_length() - 1)]


class Layer:
    def __init__(self, tp, planes):
        self.tp, self.planes = tp, planes
        self.t, self.c, self.z = (lax.axis_index(a) for a in ("tp", "core", "fsdp"))


    def hop(self, value, j):
        return lax.ppermute(value, "tp", [(i, i ^ j) for i in range(self.tp)])

    def other_core(self, value):
        return lax.ppermute(value, "core", [(0, 1), (1, 0)])

    def other_plane(self, value, k):
        return lax.ppermute(value, "fsdp", [(i, i ^ k) for i in range(self.planes)])

    def spread(self, value, bits):
        held = {0: value}
        for bit in bits:
            held.update({j | bit: self.hop(v, bit) for j, v in list(held.items())})
        return [held[j] for j in range(self.tp)]

    def gather_tp(self, halves):
        bits = bits_of(self.tp)
        left, right = self.spread(halves[0], bits), self.spread(halves[1], bits[::-1])
        return left, right

    def collect(self, parts, bits):
        held = dict(enumerate(parts))
        for bit in bits[::-1]:
            for j in [j for j in held if not j & bit]:
                came = self.hop(held[j | bit].astype(BF), bit)
                held[j] = held[j] + came.astype(F32)
                del held[j | bit]
        return held[0]

    def scatter_tp(self, partial):
        half = partial.shape[2] // 2
        bits = bits_of(self.tp)
        left = self.collect([partial[j, :, :half] for j in range(self.tp)], bits)
        right = self.collect([partial[j, :, half:] for j in range(self.tp)], bits[::-1])
        return jnp.concatenate([left, right], axis=1)

    def tp_direct(self, value):
        return jnp.stack([value] + [self.hop(value, j) for j in range(1, self.tp)])

    def tp_sum(self, value):
        total = value
        for j in range(1, self.tp):
            came = self.hop(value, j)
            total = total + jnp.stack([came[i ^ j] for i in range(self.tp)])
        return total

    def to_owner(self, stack):
        return jnp.stack([stack[0]] + [self.hop(stack[j], j) for j in range(1, self.tp)])

    def gather_cz(self, value):
        planes = jnp.stack([value] + [self.other_plane(value, k) for k in range(1, self.planes)])
        return jnp.concatenate([planes, self.other_core(planes)])


    def swap_halves(self, value):
        half = value.shape[-1] // 2
        turned = jnp.concatenate([value[..., half:], value[..., :half]], axis=-1)
        return jnp.where(self.c == 0, value, turned)

    def own_halves(self, value):
        split = value.reshape(value.shape[:-1] + (self.tp, 2, -1))
        first, second = split[..., 0, :], split[..., 1, :]
        shape = value.shape[:-1] + (value.shape[-1] // 2,)
        return (
            jnp.where(self.c == 0, first, second).reshape(shape),
            jnp.where(self.c == 0, second, first).reshape(shape),
        )

    def natural(self, value):
        split = value.reshape(value.shape[:-1] + (2, self.tp, -1))
        first, second = split[..., 0, :, :], split[..., 1, :, :]
        both = jnp.stack(
            [jnp.where(self.c == 0, first, second), jnp.where(self.c == 0, second, first)], axis=-2
        )
        return both.reshape(value.shape)


    def rings(self, block):
        lead, rows, n = block.shape
        held = jnp.zeros((2, lead, self.planes, rows, n), block.dtype)
        for k in range(self.planes):
            if k:
                block = lax.ppermute(
                    block, "fsdp", [(i, (i + 1) % self.planes) for i in range(self.planes)]
                )
            at = lax.rem(self.z + self.planes - k, self.planes)
            held = lax.dynamic_update_slice(held, block[None, :, None], (0, 0, at, 0, 0))
            held = lax.dynamic_update_slice(
                held, self.other_core(block)[None, :, None], (1, 0, at, 0, 0)
            )
        return held

    def shuffle(self, shard, blocks):
        rows = shard.shape[0]
        split = shard.reshape(rows, blocks, self.tp, -1).transpose(2, 0, 1, 3)
        return lax.all_to_all(split.reshape(self.tp, rows, -1), "tp", 0, 0, tiled=True)

    def by_columns(self, shuffled):
        return self.rings(shuffled).reshape(-1, shuffled.shape[2])

    def by_rows(self, shard):
        return self.rings(shard[None]).reshape(-1, shard.shape[1])


def attend(queries, key_heads, value_heads, bias):
    logits = jnp.einsum("bqhe,bkhe->bhqk", queries, key_heads, preferred_element_type=F32)
    probs = jax.nn.softmax(logits * HDIM ** (-0.5) + bias[:, None, None, :], axis=-1)
    mixture = jnp.einsum(
        "bhqk,bkhe->bqhe", probs.astype(BF), value_heads, preferred_element_type=F32
    )
    return probs, mixture.astype(BF)


def attend_back(queries, key_heads, value_heads, probs, grad_mix):
    grad_probs = jnp.einsum("bhe,bkhe->bhk", grad_mix, value_heads, preferred_element_type=F32)
    grad_scores = probs * (grad_probs - jnp.sum(grad_probs * probs, axis=-1, keepdims=True))
    grad_scores = grad_scores.astype(BF)
    grad_query = jnp.einsum("bhk,bkhe->bhe", grad_scores, key_heads, preferred_element_type=F32)
    return grad_scores, grad_query * HDIM ** (-0.5)


def head_blocks(rows, local):
    images = rows.shape[0]
    spread = rows.reshape(images, 1, local, HDIM) * jnp.eye(local, dtype=rows.dtype)[None, :, :, None]
    return spread.reshape(images * local, local * HDIM)


def shards(
    tp,
    planes,
    tokens,
    text,
    cotangent,
    positions,
    text_lengths,
    mask_embed,
    gain_attn,
    w_qkv,
    w_attn_out,
    gain_cross,
    w_cross_q,
    w_cross_kv,
    w_cross_out,
    gain_mlp,
    w_up,
    w_down,
):
    me = Layer(tp, planes)
    seq, width = tokens.shape
    masked_count = positions.shape[1]
    free = seq - masked_count
    txt = text.shape[1]
    local = HEADS // tp
    rows = free + PAD
    device = (me.t * 2 + me.c) * planes + me.z
    world = tp * 2 * planes
    own = width // world
    scale = HDIM ** (-0.5)

    qkv_rel = me.by_columns(me.shuffle(w_qkv, 3))
    out_rel = me.by_rows(w_attn_out)
    kv_rel = me.by_columns(me.shuffle(w_cross_kv, 2))
    cq_rel = me.by_columns(me.shuffle(w_cross_q, 1))
    cout_rel = me.by_rows(w_cross_out)
    up_rel = me.by_columns(me.shuffle(w_up, 1))
    down_rel = me.by_rows(w_down)

    vectors = jnp.stack([mask_embed, gain_attn, gain_cross, gain_mlp])
    vectors = me.tp_direct(me.gather_cz(vectors)).reshape(world, 4, own)
    vectors = xor_order(vectors, device, world)
    vectors = vectors.transpose(1, 0, 2).reshape(4, width).astype(F32)
    embed, gain_a, gain_c, gain_m = vectors[0], vectors[1], vectors[2], vectors[3]

    spots = lax.broadcasted_iota(jnp.int32, (masked_count, seq), 1)
    masked = jnp.sum((positions[0][:, None] == spots).astype(F32), axis=0)
    below = lax.broadcasted_iota(jnp.int32, (seq, seq), 0) <= lax.broadcasted_iota(
        jnp.int32, (seq, seq), 1
    )
    rank = dot((1.0 - masked).astype(BF)[None, :], below.astype(BF))[0]
    ranks = lax.broadcasted_iota(jnp.int32, (free, seq), 0).astype(F32) + 1.0
    pick = ((rank[None, :] == ranks) & (masked[None, :] == 0.0)).astype(BF)
    place = jnp.concatenate(
        [pick.T, masked[:, None].astype(BF), jnp.zeros((seq, PAD - 1), BF)], axis=1
    )
    start_free = dot(pick, tokens)
    start = jnp.concatenate([start_free, jnp.broadcast_to(embed[None], (PAD, width))])

    cot_sum = jnp.sum(cotangent[0].astype(F32), axis=0)
    cot_all = lax.all_gather(cot_sum[None], ("core", "fsdp"), axis=0, tiled=True)
    cot_group = me.tp_direct(cot_sum[None])[:, 0]
    cot_high = cot_group.astype(BF)

    cot_all = me.tp_direct(cot_all)
    cot_rows = cot_all.reshape(world, width)
    high = cot_rows.astype(BF)
    low = (cot_rows - high.astype(F32)).astype(BF)
    through = dot_t(jnp.concatenate([high, low]), w_down)
    through = through[:world] + through[world:]
    through = through.reshape(tp, 2 * planes, -1).transpose(1, 0, 2)
    through = lax.all_to_all(through, ("core", "fsdp"), 0, 0, tiled=True)
    grad_active = through.transpose(1, 0, 2).reshape(tp, -1)

    text_left, text_right = me.gather_tp(me.own_halves(text[0]))
    text_rows = jnp.concatenate(
        [jnp.concatenate(text_left), jnp.concatenate(text_right)], axis=1
    )
    open_text = lax.broadcasted_iota(jnp.int32, (1, txt), 1) < text_lengths[:, None]
    text_bias = jnp.where(me.tp_direct(open_text.astype(F32))[:, 0] > 0, 0.0, -1e30)

    field_a, scale_a = normed(start)
    entries = (field_a * gain_a[None]).astype(BF)
    ent_left, ent_right = me.own_halves(entries)
    got_left, got_right = me.gather_tp((ent_left[:free], ent_right[:free]))
    ent_rows = jnp.concatenate(
        [
            jnp.concatenate(got_left + [ent_left[free:]]),
            jnp.concatenate(got_right + [ent_right[free:]]),
        ],
        axis=1,
    )
    packed = dot(ent_rows, qkv_rel).astype(BF)
    packed_free = packed[: tp * free].reshape(tp, free, 3, local, HDIM)
    packed_masked = packed[tp * free :].reshape(1, PAD, 3, local, HDIM)
    packed = jnp.concatenate(
        [packed_free, jnp.broadcast_to(packed_masked, (tp,) + packed_masked.shape[1:])], axis=1
    )
    queries, key_heads, value_heads = packed[:, :, 0], packed[:, :, 1], packed[:, :, 2]
    spot = lax.broadcasted_iota(jnp.int32, (1, rows), 1)
    key_bias = jnp.where(
        spot < free, 0.0, jnp.where(spot == free, jnp.log(float(masked_count)), -1e30)
    )
    probs, mixture = attend(queries, key_heads, value_heads, key_bias)
    mixture = mixture.reshape(tp, rows, local * HDIM)
    added = dot(me.swap_halves(mixture).reshape(tp * rows, -1), out_rel)
    after_attn = start + me.scatter_tp(added.reshape(tp, rows, width))

    field_c, scale_c = normed(after_attn)
    cross_entries = (field_c * gain_c[None]).astype(BF)
    got_left, got_right = me.gather_tp(me.own_halves(cross_entries))
    cross_rows = jnp.concatenate([jnp.concatenate(got_left), jnp.concatenate(got_right)], axis=1)
    cross_queries = dot(cross_rows, cq_rel).astype(BF).reshape(tp, rows, local, HDIM)
    pair = dot(text_rows, kv_rel).astype(BF).reshape(tp, txt, 2, local, HDIM)
    text_keys, text_values = pair[:, :, 0], pair[:, :, 1]
    cross_probs, cross_mix = attend(cross_queries, text_keys, text_values, text_bias)
    cross_mix = cross_mix.reshape(tp, rows, local * HDIM)
    added = dot(me.swap_halves(cross_mix).reshape(tp * rows, -1), cout_rel)
    after_cross = after_attn + me.scatter_tp(added.reshape(tp, rows, width))

    field_m, scale_m = normed(after_cross)
    mlp_entries = (field_m * gain_m[None]).astype(BF)
    got_left, got_right = me.gather_tp(me.own_halves(mlp_entries))
    mlp_rows = jnp.concatenate([jnp.concatenate(got_left), jnp.concatenate(got_right)], axis=1)
    hidden = dot(mlp_rows, up_rel)
    active = jax.nn.gelu(hidden).astype(BF)
    added = dot(me.swap_halves(active), down_rel)
    output = after_cross + me.scatter_tp(added.reshape(tp, rows, width))
    output = dot(place, output.astype(BF)).astype(BF)

    field_c1, scale_c1 = normed(me.tp_direct(after_attn[free]))
    field_m1, scale_m1 = normed(me.tp_direct(after_cross[free]))

    hidden_one = hidden.reshape(tp, rows, -1)[:, free]
    active_one, gelu_back = jax.vjp(jax.nn.gelu, hidden_one)
    active_one = active_one.astype(BF)
    grad_pre = gelu_back(grad_active)[0].astype(BF)
    grad_entry = me.natural(me.tp_sum(dot_t(grad_pre, up_rel)))
    grad_gain_m = grad_entry[0] * field_m1[0]
    grad_mid = cot_group + norm_back(grad_entry * gain_m[None], field_m1, scale_m1)
    low_mid = grad_mid.astype(BF)

    grad_cmix = me.swap_halves(dot_t(low_mid, cout_rel)).astype(BF)
    query_one = cross_queries[:, free]
    cross_probs_one = cross_probs[:, :, free]
    grad_scores, grad_cq = attend_back(
        query_one, text_keys, text_values, cross_probs_one, grad_cmix.reshape(tp, local, HDIM)
    )
    grad_cq = grad_cq.reshape(tp, -1).astype(BF)
    query_one = query_one.reshape(tp, -1)
    grad_entry = me.natural(me.tp_sum(dot_t(grad_cq, cq_rel)))
    grad_gain_c = grad_entry[0] * field_c1[0]
    grad_attn = grad_mid + norm_back(grad_entry * gain_c[None], field_c1, scale_c1)
    low_attn = grad_attn.astype(BF)

    heads_back = jnp.concatenate(
        [
            jnp.pad(head_blocks(query_one, local), ((0, 0), (0, local * HDIM))),
            jnp.pad(head_blocks(grad_cmix, local), ((0, 0), (local * HDIM, 0))),
        ]
    )
    rows_back = dot_t(heads_back, kv_rel).reshape(2, tp, local, width)
    rows_back = jnp.stack([rows_back[0] * scale, rows_back[1]], axis=1).astype(BF)
    weighs = jnp.stack([grad_scores, cross_probs_one.astype(BF)], axis=1)
    sent = jnp.concatenate([rows_back, weighs], axis=-1).reshape(tp, 2 * local, width + txt)
    sent = me.to_owner(sent)
    weighs = sent[:, :, width:].reshape(tp * 2 * local, txt)
    rows_back = me.natural(sent[:, :, :width].reshape(tp * 2 * local, width))
    grad_text = dot_sum(weighs, rows_back).astype(BF)
    weighs = xor_order(sent[:, :, width:], me.t, tp).reshape(tp * 2 * local, txt)
    left_text = dot(weighs, text[0]).astype(BF)
    lefts = jnp.concatenate(
        [left_text, cross_entries[free : free + 1], mlp_entries[free : free + 1]]
    )
    lefts = lefts.reshape(-1, world, own).transpose(1, 0, 2)
    lefts = lax.all_to_all(lefts, ("tp", "core", "fsdp"), 0, 0, tiled=True)

    grad_amix = me.swap_halves(dot_t(low_attn, out_rel)).astype(BF)
    attn_scores, grad_q = attend_back(
        queries[:, free],
        key_heads,
        value_heads,
        probs[:, :, free],
        grad_amix.reshape(tp, local, HDIM),
    )
    grad_q = grad_q.reshape(tp, -1).astype(BF)
    span = local * HDIM
    query_zero = queries[0, free].reshape(1, -1)
    heads_back = jnp.concatenate(
        [
            jnp.pad(head_blocks(grad_amix, local), ((0, 0), (2 * span, 0))),
            jnp.pad(head_blocks(query_zero, local), ((0, 0), (span, span))),
            jnp.pad(grad_q, ((0, 0), (0, 2 * span))),
        ]
    )
    rows_back = dot_t(heads_back, qkv_rel)
    value_rows = rows_back[: tp * local].reshape(tp, local, width)
    key_rows = rows_back[tp * local : tp * local + local] * scale
    query_rows = rows_back[tp * local + local :].reshape(tp, 1, width)
    rows_back = jnp.concatenate(
        [jnp.broadcast_to(key_rows[None], (tp, local, width)), value_rows, query_rows], axis=1
    ).astype(BF)
    weighs = jnp.concatenate([attn_scores, probs[:, :, free].astype(BF)], axis=1)
    only = (lax.broadcasted_iota(jnp.int32, (tp, 1, rows), 2) == free).astype(BF)
    weighs = jnp.concatenate([weighs, only], axis=1)
    sent = me.to_owner(jnp.concatenate([rows_back, weighs], axis=-1))
    count = 2 * local + 1
    weighs = sent[:, :, width:].reshape(tp * count, rows)
    rows_back = me.natural(sent[:, :, :width].reshape(tp * count, width))
    grad_entry = dot_sum(weighs, rows_back)
    weighs = xor_order(sent[:, : 2 * local, width:], me.t, tp).reshape(tp * 2 * local, rows)
    left_attn = dot(weighs, entries)
    grad_gain_a = jnp.sum(grad_entry * field_a, axis=0)
    grad_start = norm_back(grad_entry * gain_a[None], field_a, scale_a)
    grad_embed = grad_attn[0] + grad_start[free]
    grad_tokens = dot(place[:, :free], grad_start[:free].astype(BF)).astype(BF)
    summed = jnp.stack([grad_embed, grad_gain_a, grad_gain_c, grad_gain_m])
    lefts2 = jnp.concatenate([left_attn, summed]).astype(BF)
    lefts2 = lefts2.reshape(-1, world, own).transpose(1, 0, 2)
    lefts2 = lax.all_to_all(lefts2, ("tp", "core", "fsdp"), 0, 0, tiled=True)

    mixed_one = mixture[:, free]
    cross_one = cross_mix[:, free]
    by_group = me.gather_cz(
        jnp.concatenate([mixed_one, cross_one, active_one, cot_high, low_mid, low_attn], axis=1)
    )
    by_group = by_group.reshape(world, -1)
    ff = active_one.shape[1]
    cuts = [span, 2 * span, 2 * span + ff, 2 * span + ff + width, 2 * span + ff + 2 * width]
    mixed_all, cross_all, active_all, cot_f, mid_f, attn_f = jnp.split(by_group, cuts, axis=1)
    corner = me.c * planes + me.z

    def mine(stack):
        size = stack.shape[1] // (2 * planes)
        return lax.dynamic_slice_in_dim(stack, corner * size, size, axis=1)

    grad_w_out = dot_sum(mine(mixed_all), attn_f)
    grad_w_cout = dot_sum(mine(cross_all), mid_f)
    grad_w_down = dot_sum(mine(active_all), cot_f)

    by_column = me.gather_cz(
        jnp.concatenate([grad_pre, grad_cq, query_one, grad_cmix, grad_amix, grad_q], axis=1)
    )
    query_wide = me.tp_direct(query_zero)
    pieces = []
    for j in range(tp):
        came = me.hop(by_column, j) if j else by_column
        came = jnp.stack([came[:, i ^ j] for i in range(tp)], axis=1)
        pieces.append(came.reshape(world, -1))
    by_column = xor_order(jnp.stack(pieces), me.t, tp)
    query_wide = xor_order(query_wide, me.t, tp).reshape(HEADS, HDIM)

    def columns(start_at, size):
        return by_column[:, :, start_at : start_at + size]

    def flat(part):
        return part.transpose(1, 0, 2).reshape(world, -1)

    pre_f = flat(columns(0, ff))
    cq_f = flat(columns(ff, span))
    query_f = flat(columns(ff + span, span)).reshape(world, HEADS, HDIM)
    cmix_f = flat(columns(ff + 2 * span, span)).reshape(world, HEADS, HDIM)
    amix_f = flat(columns(ff + 3 * span, span)).reshape(world, HEADS, HDIM)
    q_f = flat(columns(ff + 4 * span, span))

    def image_order(stack):
        ordered = xor_order(stack, device, world)
        ordered = ordered.reshape((tp, 2 * planes) + stack.shape[1:])
        return ordered.swapaxes(0, 1).reshape(stack.shape)

    lefts = image_order(lefts)
    text_left = lefts[:, : 2 * HEADS].reshape(world, tp, 2, local, own)
    text_left = text_left.transpose(2, 0, 1, 3, 4).reshape(2, world, HEADS, own)
    grad_w_cq = dot_sum(lefts[:, 2 * HEADS], cq_f)
    grad_w_up = dot_sum(lefts[:, 2 * HEADS + 1], pre_f)

    def by_head(left, right):
        outer = jnp.einsum("ihr,ihe->hre", left, right, preferred_element_type=F32)
        return outer.transpose(1, 0, 2).reshape(own, width)

    grad_w_kv = jnp.concatenate(
        [by_head(text_left[0], query_f) * scale, by_head(text_left[1], cmix_f)], axis=1
    )
    attn_left = image_order(lefts2[:, : 2 * HEADS]).reshape(world, tp, 2, local, own)
    attn_left = attn_left.transpose(2, 0, 1, 3, 4).reshape(2, world, HEADS, own)
    key_left = jnp.sum(attn_left[0].astype(F32), axis=0)
    entry_own = lax.dynamic_slice_in_dim(entries[free], device * own, own).astype(F32)
    query_sum = jnp.sum(q_f.astype(F32), axis=0)
    grad_k = key_left[:, :, None] * query_wide.astype(F32)[:, None, :] * scale
    grad_w_qkv = jnp.concatenate(
        [
            entry_own[:, None] * query_sum[None, :],
            grad_k.transpose(1, 0, 2).reshape(own, width),
            by_head(attn_left[1], amix_f),
        ],
        axis=1,
    )
    summed = jnp.sum(lefts2[:, 2 * HEADS :].astype(F32), axis=0)
    return (
        output,
        grad_tokens,
        grad_text[None],
        summed[0],
        summed[1],
        grad_w_qkv,
        grad_w_out,
        summed[2],
        grad_w_cq,
        grad_w_kv,
        grad_w_cout,
        summed[3],
        grad_w_up,
        grad_w_down,
    )


def solution(mesh):
    tp, planes = mesh.shape["dp"] // 2, mesh.shape["fsdp"]
    fine = Mesh(mesh.devices.reshape(tp, 2, planes), ("tp", "core", "fsdp"))
    every = ("tp", "core", "fsdp")
    one, two, three = P(every), P(every, None), P(every, None, None)

    def layer(*arguments):
        return shards(tp, planes, *arguments)

    return jax.shard_map(
        layer,
        mesh=fine,
        in_specs=(two, three, three, two, one, one, one, two, two, one, two, two, two, one, two, two),
        out_specs=(two, two, three, one, one, two, two, one, two, two, two, one, two, two),
        check_vma=False,
    )
```

time: 6080 us -> 857 us (0.14)
  waiting for transfers between devices: 5580 us -> 241 us
  matrix products: 308 us -> 93.6 us
  local copies, waits for them, and re-layouts: 62.3 us -> 254 us
  starting transfers between devices: 1.34 us -> 146 us
  other arithmetic: 11.7 us -> 78.1 us
    reduce_scatter x6 -> x0, waiting for transfers between devices: 4090 us -> none  [reduce_grads(): lax.psum_scatter(gradients, ('dp', 'fsdp'), scatter_dimension=0, tiled=True)]
    all_gather x7 -> x0, waiting for transfers between devices: 771 us -> none  [fetch_forward(): lax.all_gather(as_sent(weights), ('dp', 'fsdp'), axis=0, tiled=True)]
    unnamed x15 -> x0, waiting for transfers between devices: 718 us -> none
    ppermute x0 -> x139, waiting for transfers between devices: none -> 230 us  [the longest x21 160 us: rings(): lax.ppermute(block, 'fsdp', [(i, (i + 1) % self.planes) for i in range(se...]
    dot_general x32 -> x36, matrix products: 301 us -> 86.9 us  [the longest x13 49.7 us: dot(): return jnp.dot(left, right, preferred_element_type=F32)]
    ppermute x0 -> x139, starting transfers between devices: none -> 120 us  [the longest x78 90.7 us: hop(): return lax.ppermute(value, 'tp', [(i, i ^ j) for i in range(self.tp)])]
    unnamed x2 -> x0, blocking collectives: 86.4 us -> none
    dynamic_update_slice x0 -> x56, local copies, waits for them, and re-layouts: none -> 77.2 us  [the longest x28 39.2 us: rings(): lax.dynamic_update_slice(held, block[None, :, None], (0, 0, at, 0, 0))]
  transfers between devices with their start and end apart: 14 -> 146, of which waited for: 14 -> 47; matrix products, arithmetic and copies ran while one was open for 5% -> 48% of each run, Pallas kernels for 0% -> 0%
where the time goes in v1:
time: 857 us; the launch traced here: 844 us
  local copies, waits for them, and re-layouts  254 us (30%)
  waiting for transfers between devices  241 us (28%)
  starting transfers between devices  146 us (17%)
  matrix products  93.6 us (11%)
  other arithmetic  78.1 us (9%)
  blocking collectives  26.1 us (3%)
    ppermute x21, waiting for transfers between devices, rings(): lax.ppermute(block, 'fsdp', [(i, (i + 1) % self.planes) for i in range(se...  160 us
    ppermute x78, starting transfers between devices, hop(): return lax.ppermute(value, 'tp', [(i, i ^ j) for i in range(self.tp)])  90.7 us
    ppermute x78, waiting for transfers between devices, hop(): return lax.ppermute(value, 'tp', [(i, i ^ j) for i in range(self.tp)])  56.2 us
    dot_general x13, matrix products, dot(): return jnp.dot(left, right, preferred_element_type=F32)  49.7 us
    dynamic_update_slice x28, local copies, waits for them, and re-layouts, rings(): lax.dynamic_update_slice(held, block[None, :, None], (0, 0, at, 0, 0))  39.2 us
    dynamic_update_slice x28, local copies, waits for them, and re-layouts, rings(): lax.dynamic_update_slice(held, self.other_core(block)[None, :, None], (1,...  38 us
    unnamed x303, local copies, waits for them, and re-layouts  28 us
    all_gather x1, blocking collectives, shards(): lax.all_gather(cot_sum[None], ('core', 'fsdp'), axis=0, tiled=True)  26.1 us
  transfers between devices with their start and end apart: 146, of which 47 were waited for; matrix products, arithmetic and copies ran while one was open for 48% of the time, Pallas kernels for 0%

profile of v1, /device:TPU:0, one launch (start us, length us, event | category | flops | bytes accessed | tf_op | source)
XLA Modules:
  0.0 843.7 jit_solution(6965788431222409742)
XLA Ops:
  1.5 3.1 collective-permute-start
  4.6 2.6 collective-permute-start.1
  10.6 26.1 %all-gather = f32[16384]{0:T(1024)S(1)} all-gather(f32[2048]{0:T(1024)S(1)} %convert_reduce_fusion), channel_id=2, replica_groups=mesh['tp'=4,'core'=2,'fsdp'=4] {'core','fsdp'}, dimensions={0}, use_global_device_ids=true | all-gather | bytes 73728 | tf_op jit(solution)/shard_map/all_gather | solution.py:246
  42.6 2.7 reshape.1752
  46.7 3.5 reshape.1753
  56.9 2.6 reshape.1768
  59.5 2.8 copy.565
  69.5 4.3 broadcast_in_dim.334
  98.4 4.0 all-to-all-start.4
  102.5 5.6 all-to-all-done.4
  108.2 3.9 all-to-all-start.2
  122.0 4.2 all-to-all-start.1
  148.7 3.5 all-to-all-start
  157.4 3.1 collective-permute-done.53
  165.2 4.1 collective-permute-done.23
  171.4 3.4 collective-permute-done.65
  178.5 4.3 collective-permute-done.9
  184.3 3.5 all-to-all-start.3
  187.9 3.4 broadcast_in_dim.276
  199.5 8.5 %collective-permute-done.25 = bf16[1,64,2048]{2,1,0:T(8,128)(2,1)S(1)} collective-permute-done((bf16[1,64,2048]{2,1,0:T(8,128)(2,1)S(1)}, bf16[1,64,2048]{2,1,0:T(8,128)(2,1)S(1)}, u32[]{:S(2)}, u32[]{:S(2)}) %collective-permute-start.25) | collective-permute-done | bytes 262176 | tf_op jit(solution)/shard_map/ppermute | solution.py:140
  208.8 8.8 %collective-permute-done.67 = bf16[1,64,2048]{2,1,0:T(8,128)(2,1)S(1)} collective-permute-done((bf16[1,64,2048]{2,1,0:T(8,128)(2,1)S(1)}, bf16[1,64,2048]{2,1,0:T(8,128)(2,1)S(1)}, u32[]{:S(2)}, u32[]{:S(2)}) %collective-permute-start.67) | collective-permute-done | bytes 262176 | tf_op jit(solution)/shard_map/ppermute | solution.py:140
  219.0 4.3 broadcast_in_dim.325
  226.4 5.6 collective-permute-done.40
  234.6 5.8 collective-permute-done.57
  251.2 11.1 %collective-permute-done.14 = bf16[4,64,1536]{2,1,0:T(8,128)(2,1)S(1)} collective-permute-done((bf16[4,64,1536]{2,1,0:T(8,128)(2,1)S(1)}, bf16[4,64,1536]{2,1,0:T(8,128)(2,1)S(1)}, u32[]{:S(2)}, u32[]{:S(2)}) %collective-permute-start.14) | collective-permute-done | bytes 786464 | tf_op jit(solution)/shard_map/ppermute | solution.py:140
  264.1 27.8 %collective-permute-done.42 = bf16[4,64,1024]{2,1,0:T(8,128)(2,1)S(1)} collective-permute-done((bf16[4,64,1024]{2,1,0:T(8,128)(2,1)}, bf16[4,64,1024]{2,1,0:T(8,128)(2,1)S(1)}, u32[]{:S(2)}, u32[]{:S(2)}) %collective-permute-start.42) | collective-permute-done | bytes 524320 | tf_op jit(solution)/shard_map/ppermute | solution.py:140
  299.1 27.2 %collective-permute-done.44 = bf16[4,64,1024]{2,1,0:T(8,128)(2,1)S(1)} collective-permute-done((bf16[4,64,1024]{2,1,0:T(8,128)(2,1)S(1)}, bf16[4,64,1024]{2,1,0:T(8,128)(2,1)S(1)}, u32[]{:S(2)}, u32[]{:S(2)}) %collective-permute-start.44) | collective-permute-done | bytes 524320 | tf_op jit(solution)/shard_map/ppermute | solution.py:140
  336.0 16.0 %collective-permute-done.16 = bf16[4,64,1536]{2,1,0:T(8,128)(2,1)S(1)} collective-permute-done((bf16[4,64,1536]{2,1,0:T(8,128)(2,1)S(1)}, bf16[4,64,1536]{2,1,0:T(8,128)(2,1)S(1)}, u32[]{:S(2)}, u32[]{:S(2)}) %collective-permute-start.16) | collective-permute-done | bytes 786464 | tf_op jit(solution)/shard_map/ppermute | solution.py:140
  355.8 4.1 collective-permute-done.38
  359.9 5.7 fusion.75
  368.7 14.6 %collective-permute-done.84 = bf16[4,64,2048]{2,1,0:T(8,128)(2,1)} collective-permute-done((bf16[4,64,2048]{2,1,0:T(8,128)(2,1)}, bf16[4,64,2048]{2,1,0:T(8,128)(2,1)}, u32[]{:S(2)}, u32[]{:S(2)}) %collective-permute-start.84) | collective-permute-done | bytes 1048608 | tf_op jit(solution)/shard_map/ppermute | solution.py:140
  388.0 10.3 %collective-permute-start.86 = (bf16[4,64,2048]{2,1,0:T(8,128)(2,1)}, bf16[4,64,2048]{2,1,0:T(8,128)(2,1)}, u32[]{:S(2)}, u32[]{:S(2)}) collective-permute-start(bf16[4,64,2048]{2,1,0:T(8,128)(2,1)} %collective-permute-done.84), channel_id=1, source_target_pairs={{0,1},{1,2},{2,3},{3,0},{4,5},{5,6},{6,7},{7,4},{8,9},{9,10},{10,1... | collective-permute-start | bytes 3145736 | tf_op jit(solution)/shard_map/ppermute | solution.py:140
  398.3 24.2 %collective-permute-done.18 = bf16[4,64,1536]{2,1,0:T(8,128)(2,1)S(1)} collective-permute-done((bf16[4,64,1536]{2,1,0:T(8,128)(2,1)S(1)}, bf16[4,64,1536]{2,1,0:T(8,128)(2,1)S(1)}, u32[]{:S(2)}, u32[]{:S(2)}) %collective-permute-start.18) | collective-permute-done | bytes 786464 | tf_op jit(solution)/shard_map/ppermute | solution.py:140
  431.3 6.8 convolution_convert_fusion
  443.7 2.9 collective-permute-start.134
  446.6 3.0 fusion.356
  464.9 5.3 fusion.359
  478.2 6.6 collective-permute-done.28
  491.2 3.5 collective-permute-done.31
  494.7 6.3 collective-permute-done.29
  520.4 2.6 multiply_reduce_fusion.3
  549.8 4.4 fusion.80
  555.9 3.7 fusion.360
  574.7 3.1 fusion.363
  583.7 4.8 collective-permute-done.70
  594.5 4.2 collective-permute-done.71
  610.7 3.0 fusion.331
  621.9 2.5 multiply_reduce_fusion.2
  627.5 3.5 fusion.72
  655.5 9.8 %fusion.11 = (bf16[576,2048]{1,0:T(8,128)(2,1)S(1)}, f32[576,2048]{1,0:T(8,128)S(1)}) fusion(bf16[2048,2048]{1,0:T(8,128)(2,1)} %bitcast.152, bf16[144,1024]{1,0:T(8,128)(2,1)S(1)} %collective-permute-done.80, bf16[144,1024]{1,0:T(8,128)(2,1)S(1)} %collective-permute-done.79, bf16[144,1024]{1,0:T(8,128)(2,1)} %collective-permute-done.78, ...), kind=kOutput, calls=%fused_computation.12 | convolution fusion | flops 4861329408 | bytes 17825792 | tf_op jit(solution)/shard_map/dot_general | solution.py:14
  666.2 5.6 fusion.368
  676.6 10.3 %fusion.364 = (bf16[4,144,2048]{2,1,0:T(8,128)(2,1)S(1)}, f32[4,144,2048]{2,1,0:T(8,128)}) fusion(bf16[4,144,2048]{2,1,0:T(8,128)(2,1)S(1)} %bitcast.843, bf16[2048,2048,1]{1,0,2:T(8,128)(2,1)} %bitcast.172), kind=kOutput, calls=%fused_computation.703 | convolution fusion | flops 4833017856 | bytes 17825792 | tf_op jit(solution)/shard_map/dot_general | solution.py:14
  720.0 3.5 fusion.186
  725.9 4.6 fusion.365
  744.1 3.6 all-to-all-start.6
  766.0 2.7 collective-permute-start.136
  768.7 4.0 collective-permute-done.136
  773.7 5.4 collective-permute-done.137
  783.1 3.0 all-to-all-start.5
  789.5 5.2 all-to-all-done.5
  805.9 3.8 collective-permute-done.130
  809.6 2.7 collective-permute-start.97
  816.7 6.3 rev.76
  837.3 2.6 fusion.271
  (971 shorter events, 434.8 us)
Async XLA Ops:
  1.5 75.9 %collective-permute-start = (bf16[4,64]{1,0:T(4,128)(2,1)S(1)}, bf16[4,64]{1,0:T(4,128)(2,1)S(1)}, u32[]{:S(2)}, u32[]{:S(2)}) collective-permute-start(bf16[4,64]{1,0:T(4,128)(2,1)S(1)} %get-tuple-element.40), channel_id=1, source_target_pairs={{0,1},{1,0},{2,3},{3,2},{4,5},{5,4},{6,7},{7,6},{8,9},{9,8},{10,11... | collective-permute-start | bytes 1544 | tf_op jit(solution)/shard_map/ppermute | solution.py:65
  4.6 74.3 %collective-permute-start.1 = (bf16[4,64]{1,0:T(4,128)(2,1)S(1)}, bf16[4,64]{1,0:T(4,128)(2,1)S(1)}, u32[]{:S(2)}, u32[]{:S(2)}) collective-permute-start(bf16[4,64]{1,0:T(4,128)(2,1)S(1)} %get-tuple-element.40), channel_id=1, source_target_pairs={{0,2},{1,3},{2,0},{3,1},{4,6},{5,7},{6,4},{7,5},{8,10},{9,11},{10,... | collective-permute-start | bytes 1544 | tf_op jit(solution)/shard_map/ppermute | solution.py:65
  7.1 73.2 %collective-permute-start.2 = (bf16[4,64]{1,0:T(4,128)(2,1)S(1)}, bf16[4,64]{1,0:T(4,128)(2,1)S(1)}, u32[]{:S(2)}, u32[]{:S(2)}) collective-permute-start(bf16[4,64]{1,0:T(4,128)(2,1)S(1)} %get-tuple-element.40), channel_id=1, source_target_pairs={{0,3},{1,2},{2,1},{3,0},{4,7},{5,6},{6,5},{7,4},{8,11},{9,10},{10,... | collective-permute-start | bytes 1544 | tf_op jit(solution)/shard_map/ppermute | solution.py:65
  7.1 121.3 %collective-permute-start.20 = (bf16[1,64,2048]{2,1,0:T(8,128)(2,1)}, bf16[1,64,2048]{2,1,0:T(8,128)(2,1)}, u32[]{:S(2)}, u32[]{:S(2)}) collective-permute-start(bf16[1,64,2048]{2,1,0:T(8,128)(2,1)} %bitcast.902), channel_id=1, source_target_pairs={{0,4},{4,0},{1,5},{5,1},{2,6},{6,2},{3,7},{7,3},{8,12},{12,8},{9,1... | collective-permute-start | bytes 786440 | tf_op jit(solution)/shard_map/ppermute | solution.py:62
  7.2 127.1 %collective-permute-start.21 = (bf16[1,64,2048]{2,1,0:T(8,128)(2,1)}, bf16[1,64,2048]{2,1,0:T(8,128)(2,1)}, u32[]{:S(2)}, u32[]{:S(2)}) collective-permute-start(bf16[1,64,2048]{2,1,0:T(8,128)(2,1)} %bitcast.903), channel_id=1, source_target_pairs={{0,1},{1,2},{2,3},{3,0},{4,5},{5,6},{6,7},{7,4},{8,9},{9,10},{10,1... | collective-permute-start | bytes 786440 | tf_op jit(solution)/shard_map/ppermute | solution.py:140
  94.5 36.1 %collective-permute-start.62 = (bf16[1,64,2048]{2,1,0:T(8,128)(2,1)}, bf16[1,64,2048]{2,1,0:T(8,128)(2,1)}, u32[]{:S(2)}, u32[]{:S(2)}) collective-permute-start(bf16[1,64,2048]{2,1,0:T(8,128)(2,1)} %bitcast.115), channel_id=1, source_target_pairs={{0,4},{4,0},{1,5},{5,1},{2,6},{6,2},{3,7},{7,3},{8,12},{12,8},{9,1... | collective-permute-start | bytes 786440 | tf_op jit(solution)/shard_map/ppermute | solution.py:62
  94.6 42.8 %collective-permute-start.63 = (bf16[1,64,2048]{2,1,0:T(8,128)(2,1)}, bf16[1,64,2048]{2,1,0:T(8,128)(2,1)}, u32[]{:S(2)}, u32[]{:S(2)}) collective-permute-start(bf16[1,64,2048]{2,1,0:T(8,128)(2,1)} %bitcast.115), channel_id=1, source_target_pairs={{0,1},{1,2},{2,3},{3,0},{4,5},{5,6},{6,7},{7,4},{8,9},{9,10},{10,1... | collective-permute-start | bytes 786440 | tf_op jit(solution)/shard_map/ppermute | solution.py:140
  96.0 145.1 %collective-permute-start.88 = (bf16[1,256,2048]{2,1,0:T(8,128)(2,1)}, bf16[1,256,2048]{2,1,0:T(8,128)(2,1)}, u32[]{:S(2)}, u32[]{:S(2)}) collective-permute-start(bf16[1,256,2048]{2,1,0:T(8,128)(2,1)} %bitcast.156), channel_id=1, source_target_pairs={{0,4},{4,0},{1,5},{5,1},{2,6},{6,2},{3,7},{7,3},{8,12},{12,8},{9,1... | collective-permute-start | bytes 3145736 | tf_op jit(solution)/shard_map/ppermute | solution.py:62
  122.0 26.7 %all-to-all-start.1 = ((bf16[4,64,1024]{2,1,0:T(8,128)(2,1)}), bf16[4,64,1024]{2,1,0:T(8,128)(2,1)S(1)}, u32[]{:S(2)}, u32[]{:S(2)}) async-start(bf16[4,64,1024]{2,1,0:T(8,128)(2,1)} %reshape.1759), calls=%async_computation.1 | async-start | bytes 1048576 | tf_op jit(solution)/shard_map/all_to_all | solution.py:153
  128.4 115.0 %collective-permute-start.89 = (bf16[1,256,2048]{2,1,0:T(8,128)(2,1)}, bf16[1,256,2048]{2,1,0:T(8,128)(2,1)}, u32[]{:S(2)}, u32[]{:S(2)}) collective-permute-start(bf16[1,256,2048]{2,1,0:T(8,128)(2,1)} %bitcast.156), channel_id=1, source_target_pairs={{0,1},{1,2},{2,3},{3,0},{4,5},{5,6},{6,7},{7,4},{8,9},{9,10},{10,1... | collective-permute-start | bytes 3145736 | tf_op jit(solution)/shard_map/ppermute | solution.py:140
  143.1 190.8 %collective-permute-start.33 = (bf16[128,1024]{0,1:T(8,128)(2,1)}, bf16[128,1024]{0,1:T(8,128)(2,1)}, u32[]{:S(2)}, u32[]{:S(2)}) collective-permute-start(bf16[128,1024]{0,1:T(8,128)(2,1)} %bitcast.68), channel_id=1, source_target_pairs={{0,8},{8,0},{16,24},{24,16},{1,9},{9,1},{17,25},{25,17},{2,10},{10... | collective-permute-start | bytes 786440 | tf_op jit(solution)/shard_map/ppermute | solution.py:59
  148.7 35.6 %all-to-all-start = ((bf16[4,64,1536]{2,1,0:T(8,128)(2,1)}), bf16[4,64,1536]{2,1,0:T(8,128)(2,1)S(1)}, u32[]{:S(2)}, u32[]{:S(2)}) async-start(bf16[4,64,1536]{2,1,0:T(8,128)(2,1)} %reshape.1753), calls=%async_computation | async-start | bytes 1572864 | tf_op jit(solution)/shard_map/all_to_all | solution.py:153
  177.1 15.1 %collective-permute-start.54 = (bf16[4,64,512]{2,1,0:T(8,128)(2,1)}, bf16[4,64,512]{2,1,0:T(8,128)(2,1)}, u32[]{:S(2)}, u32[]{:S(2)}) collective-permute-start(bf16[4,64,512]{2,1,0:T(8,128)(2,1)} %collective-permute-done.53), channel_id=1, source_target_pairs={{0,4},{4,0},{1,5},{5,1},{2,6},{6,2},{3,7},{7,3},{8,12},{12,8},{9,1... | collective-permute-start | bytes 786440 | tf_op jit(solution)/shard_map/ppermute | solution.py:62
  184.3 34.7 %all-to-all-start.3 = ((bf16[4,64,2048]{2,1,0:T(8,128)(2,1)}), bf16[4,64,2048]{2,1,0:T(8,128)(2,1)S(1)}, u32[]{:S(2)}, u32[]{:S(2)}) async-start(bf16[4,64,2048]{2,1,0:T(8,128)(2,1)} %copy.565), calls=%async_computation.3 | async-start | bytes 2097152 | tf_op jit(solution)/shard_map/all_to_all | solution.py:153
  193.9 30.5 %collective-permute-start.39 = (bf16[4,64,1024]{2,1,0:T(8,128)(2,1)S(1)}, bf16[4,64,1024]{2,1,0:T(8,128)(2,1)}, u32[]{:S(2)}, u32[]{:S(2)}) collective-permute-start(bf16[4,64,1024]{2,1,0:T(8,128)(2,1)S(1)} %all-to-all-done.1), channel_id=1, source_target_pairs={{0,4},{4,0},{1,5},{5,1},{2,6},{6,2},{3,7},{7,3},{8,12},{12,8},{9,1... | collective-permute-start | bytes 1572872 | tf_op jit(solution)/shard_map/ppermute | solution.py:62
  217.6 14.4 %collective-permute-start.40 = (bf16[4,64,1024]{2,1,0:T(8,128)(2,1)S(1)}, bf16[4,64,1024]{2,1,0:T(8,128)(2,1)}, u32[]{:S(2)}, u32[]{:S(2)}) collective-permute-start(bf16[4,64,1024]{2,1,0:T(8,128)(2,1)S(1)} %all-to-all-done.1), channel_id=1, source_target_pairs={{0,1},{1,2},{2,3},{3,0},{4,5},{5,6},{6,7},{7,4},{8,9},{9,10},{10,1... | collective-permute-start | bytes 1572872 | tf_op jit(solution)/shard_map/ppermute | solution.py:140
  233.9 16.2 %collective-permute-start.13 = (bf16[4,64,1536]{2,1,0:T(8,128)(2,1)S(1)}, bf16[4,64,1536]{2,1,0:T(8,128)(2,1)S(1)}, u32[]{:S(2)}, u32[]{:S(2)}) collective-permute-start(bf16[4,64,1536]{2,1,0:T(8,128)(2,1)S(1)} %all-to-all-done), channel_id=1, source_target_pairs={{0,4},{4,0},{1,5},{5,1},{2,6},{6,2},{3,7},{7,3},{8,12},{12,8},{9,1... | collective-permute-start | bytes 2359304 | tf_op jit(solution)/shard_map/ppermute | solution.py:62
  240.4 21.9 %collective-permute-start.14 = (bf16[4,64,1536]{2,1,0:T(8,128)(2,1)S(1)}, bf16[4,64,1536]{2,1,0:T(8,128)(2,1)S(1)}, u32[]{:S(2)}, u32[]{:S(2)}) collective-permute-start(bf16[4,64,1536]{2,1,0:T(8,128)(2,1)S(1)} %all-to-all-done), channel_id=1, source_target_pairs={{0,1},{1,2},{2,3},{3,0},{4,5},{5,6},{6,7},{7,4},{8,9},{9,10},{10,1... | collective-permute-start | bytes 2359304 | tf_op jit(solution)/shard_map/ppermute | solution.py:140
  246.3 46.5 %collective-permute-start.81 = (bf16[4,64,2048]{2,1,0:T(8,128)(2,1)S(1)}, bf16[4,64,2048]{2,1,0:T(8,128)(2,1)S(1)}, u32[]{:S(2)}, u32[]{:S(2)}) collective-permute-start(bf16[4,64,2048]{2,1,0:T(8,128)(2,1)S(1)} %all-to-all-done.3), channel_id=1, source_target_pairs={{0,4},{4,0},{1,5},{5,1},{2,6},{6,2},{3,7},{7,3},{8,12},{12,8},{9,1... | collective-permute-start | bytes 3145736 | tf_op jit(solution)/shard_map/ppermute | solution.py:62
  249.3 44.5 %collective-permute-start.82 = (bf16[4,64,2048]{2,1,0:T(8,128)(2,1)S(1)}, bf16[4,64,2048]{2,1,0:T(8,128)(2,1)}, u32[]{:S(2)}, u32[]{:S(2)}) collective-permute-start(bf16[4,64,2048]{2,1,0:T(8,128)(2,1)S(1)} %all-to-all-done.3), channel_id=1, source_target_pairs={{0,1},{1,2},{2,3},{3,0},{4,5},{5,6},{6,7},{7,4},{8,9},{9,10},{10,1... | collective-permute-start | bytes 3145736 | tf_op jit(solution)/shard_map/ppermute | solution.py:140
  262.3 29.7 %collective-permute-start.42 = (bf16[4,64,1024]{2,1,0:T(8,128)(2,1)}, bf16[4,64,1024]{2,1,0:T(8,128)(2,1)S(1)}, u32[]{:S(2)}, u32[]{:S(2)}) collective-permute-start(bf16[4,64,1024]{2,1,0:T(8,128)(2,1)} %collective-permute-done.40), channel_id=1, source_target_pairs={{0,1},{1,2},{2,3},{3,0},{4,5},{5,6},{6,7},{7,4},{8,9},{9,10},{10,1... | collective-permute-start | bytes 1572872 | tf_op jit(solution)/shard_map/ppermute | solution.py:140
  263.2 65.9 %collective-permute-start.90 = (bf16[1,256,2048]{2,1,0:T(8,128)(2,1)}, bf16[1,256,2048]{2,1,0:T(8,128)(2,1)S(1)}, u32[]{:S(2)}, u32[]{:S(2)}) collective-permute-start(bf16[1,256,2048]{2,1,0:T(8,128)(2,1)} %collective-permute-done.89), channel_id=1, source_target_pairs={{0,4},{4,0},{1,5},{5,1},{2,6},{6,2},{3,7},{7,3},{8,12},{12,8},{9,1... | collective-permute-start | bytes 3145736 | tf_op jit(solution)/shard_map/ppermute | solution.py:62
  291.9 38.3 %collective-permute-start.91 = (bf16[1,256,2048]{2,1,0:T(8,128)(2,1)}, bf16[1,256,2048]{2,1,0:T(8,128)(2,1)}, u32[]{:S(2)}, u32[]{:S(2)}) collective-permute-start(bf16[1,256,2048]{2,1,0:T(8,128)(2,1)} %collective-permute-done.89), channel_id=1, source_target_pairs={{0,1},{1,2},{2,3},{3,0},{4,5},{5,6},{6,7},{7,4},{8,9},{9,10},{10,1... | collective-permute-start | bytes 3145736 | tf_op jit(solution)/shard_map/ppermute | solution.py:140
  293.8 32.5 %collective-permute-start.44 = (bf16[4,64,1024]{2,1,0:T(8,128)(2,1)S(1)}, bf16[4,64,1024]{2,1,0:T(8,128)(2,1)S(1)}, u32[]{:S(2)}, u32[]{:S(2)}) collective-permute-start(bf16[4,64,1024]{2,1,0:T(8,128)(2,1)S(1)} %collective-permute-done.42), channel_id=1, source_target_pairs={{0,1},{1,2},{2,3},{3,0},{4,5},{5,6},{6,7},{7,4},{8,9},{9,10},{10,1... | collective-permute-start | bytes 1572872 | tf_op jit(solution)/shard_map/ppermute | solution.py:140
  296.2 59.0 %collective-permute-start.34 = (bf16[128,1024]{0,1:T(8,128)(2,1)}, bf16[128,1024]{0,1:T(8,128)(2,1)S(1)}, u32[]{:S(2)}, u32[]{:S(2)}) collective-permute-start(bf16[128,1024]{0,1:T(8,128)(2,1)} %bitcast.68), channel_id=1, source_target_pairs={{0,16},{8,24},{16,0},{24,8},{1,17},{9,25},{17,1},{25,9},{2,18},{10... | collective-permute-start | bytes 786440 | tf_op jit(solution)/shard_map/ppermute | solution.py:59
  330.2 21.8 %collective-permute-start.16 = (bf16[4,64,1536]{2,1,0:T(8,128)(2,1)S(1)}, bf16[4,64,1536]{2,1,0:T(8,128)(2,1)S(1)}, u32[]{:S(2)}, u32[]{:S(2)}) collective-permute-start(bf16[4,64,1536]{2,1,0:T(8,128)(2,1)S(1)} %collective-permute-done.14), channel_id=1, source_target_pairs={{0,1},{1,2},{2,3},{3,0},{4,5},{5,6},{6,7},{7,4},{8,9},{9,10},{10,1... | collective-permute-start | bytes 2359304 | tf_op jit(solution)/shard_map/ppermute | solution.py:140
  332.5 21.9 %collective-permute-start.45 = (bf16[4,64,1024]{2,1,0:T(8,128)(2,1)S(1)}, bf16[4,64,1024]{2,1,0:T(8,128)(2,1)S(1)}, u32[]{:S(2)}, u32[]{:S(2)}) collective-permute-start(bf16[4,64,1024]{2,1,0:T(8,128)(2,1)S(1)} %collective-permute-done.44), channel_id=1, source_target_pairs={{0,4},{4,0},{1,5},{5,1},{2,6},{6,2},{3,7},{7,3},{8,12},{12,8},{9,1... | collective-permute-start | bytes 1572872 | tf_op jit(solution)/shard_map/ppermute | solution.py:62
  334.0 21.3 %collective-permute-start.36 = (bf16[128,1024]{0,1:T(8,128)(2,1)S(1)}, bf16[128,1024]{0,1:T(8,128)(2,1)S(1)}, u32[]{:S(2)}, u32[]{:S(2)}) collective-permute-start(bf16[128,1024]{0,1:T(8,128)(2,1)S(1)} %bitcast.905), channel_id=1, source_target_pairs={{0,8},{8,0},{16,24},{24,16},{1,9},{9,1},{17,25},{25,17},{2,10},{10... | collective-permute-start | bytes 786440 | tf_op jit(solution)/shard_map/ppermute | solution.py:59
  335.4 20.4 %collective-permute-start.35 = (bf16[128,1024]{0,1:T(8,128)(2,1)}, bf16[128,1024]{0,1:T(8,128)(2,1)S(1)}, u32[]{:S(2)}, u32[]{:S(2)}) collective-permute-start(bf16[128,1024]{0,1:T(8,128)(2,1)} %collective-permute-done.33), channel_id=1, source_target_pairs={{0,16},{8,24},{16,0},{24,8},{1,17},{9,25},{17,1},{25,9},{2,18},{10... | collective-permute-start | bytes 786440 | tf_op jit(solution)/shard_map/ppermute | solution.py:59
  355.2 28.1 %collective-permute-start.84 = (bf16[4,64,2048]{2,1,0:T(8,128)(2,1)}, bf16[4,64,2048]{2,1,0:T(8,128)(2,1)}, u32[]{:S(2)}, u32[]{:S(2)}) collective-permute-start(bf16[4,64,2048]{2,1,0:T(8,128)(2,1)} %collective-permute-done.82), channel_id=1, source_target_pairs={{0,1},{1,2},{2,3},{3,0},{4,5},{5,6},{6,7},{7,4},{8,9},{9,10},{10,1... | collective-permute-start | bytes 3145736 | tf_op jit(solution)/shard_map/ppermute | solution.py:140
  355.2 70.4 %collective-permute-start.92 = (bf16[1,256,2048]{2,1,0:T(8,128)(2,1)}, bf16[1,256,2048]{2,1,0:T(8,128)(2,1)}, u32[]{:S(2)}, u32[]{:S(2)}) collective-permute-start(bf16[1,256,2048]{2,1,0:T(8,128)(2,1)} %collective-permute-done.91), channel_id=1, source_target_pairs={{0,4},{4,0},{1,5},{5,1},{2,6},{6,2},{3,7},{7,3},{8,12},{12,8},{9,1... | collective-permute-start | bytes 3145736 | tf_op jit(solution)/shard_map/ppermute | solution.py:62
  355.8 72.1 %collective-permute-start.93 = (bf16[1,256,2048]{2,1,0:T(8,128)(2,1)}, bf16[1,256,2048]{2,1,0:T(8,128)(2,1)}, u32[]{:S(2)}, u32[]{:S(2)}) collective-permute-start(bf16[1,256,2048]{2,1,0:T(8,128)(2,1)} %collective-permute-done.91), channel_id=1, source_target_pairs={{0,1},{1,2},{2,3},{3,0},{4,5},{5,6},{6,7},{7,4},{8,9},{9,10},{10,1... | collective-permute-start | bytes 3145736 | tf_op jit(solution)/shard_map/ppermute | solution.py:140
  359.9 28.1 %collective-permute-start.17 = (bf16[4,64,1536]{2,1,0:T(8,128)(2,1)S(1)}, bf16[4,64,1536]{2,1,0:T(8,128)(2,1)}, u32[]{:S(2)}, u32[]{:S(2)}) collective-permute-start(bf16[4,64,1536]{2,1,0:T(8,128)(2,1)S(1)} %collective-permute-done.16), channel_id=1, source_target_pairs={{0,4},{4,0},{1,5},{5,1},{2,6},{6,2},{3,7},{7,3},{8,12},{12,8},{9,1... | collective-permute-start | bytes 2359304 | tf_op jit(solution)/shard_map/ppermute | solution.py:62
  368.7 53.8 %collective-permute-start.18 = (bf16[4,64,1536]{2,1,0:T(8,128)(2,1)S(1)}, bf16[4,64,1536]{2,1,0:T(8,128)(2,1)S(1)}, u32[]{:S(2)}, u32[]{:S(2)}) collective-permute-start(bf16[4,64,1536]{2,1,0:T(8,128)(2,1)S(1)} %collective-permute-done.16), channel_id=1, source_target_pairs={{0,1},{1,2},{2,3},{3,0},{4,5},{5,6},{6,7},{7,4},{8,9},{9,10},{10,1... | collective-permute-start | bytes 2359304 | tf_op jit(solution)/shard_map/ppermute | solution.py:140
  383.3 103.3 %collective-permute-start.85 = (bf16[4,64,2048]{2,1,0:T(8,128)(2,1)}, bf16[4,64,2048]{2,1,0:T(8,128)(2,1)}, u32[]{:S(2)}, u32[]{:S(2)}) collective-permute-start(bf16[4,64,2048]{2,1,0:T(8,128)(2,1)} %collective-permute-done.84), channel_id=1, source_target_pairs={{0,4},{4,0},{1,5},{5,1},{2,6},{6,2},{3,7},{7,3},{8,12},{12,8},{9,1... | collective-permute-start | bytes 3145736 | tf_op jit(solution)/shard_map/ppermute | solution.py:62
  388.0 115.9 %collective-permute-start.86 = (bf16[4,64,2048]{2,1,0:T(8,128)(2,1)}, bf16[4,64,2048]{2,1,0:T(8,128)(2,1)}, u32[]{:S(2)}, u32[]{:S(2)}) collective-permute-start(bf16[4,64,2048]{2,1,0:T(8,128)(2,1)} %collective-permute-done.84), channel_id=1, source_target_pairs={{0,1},{1,2},{2,3},{3,0},{4,5},{5,6},{6,7},{7,4},{8,9},{9,10},{10,1... | collective-permute-start | bytes 3145736 | tf_op jit(solution)/shard_map/ppermute | solution.py:140
  443.2 31.4 %collective-permute-start.132 = (bf16[1,512]{1,0:T(2,128)(2,1)}, bf16[1,512]{1,0:T(2,128)(2,1)}, u32[]{:S(2)}, u32[]{:S(2)}) collective-permute-start(bf16[1,512]{1,0:T(2,128)(2,1)} %get-tuple-element.83), channel_id=1, source_target_pairs={{0,8},{8,0},{16,24},{24,16},{1,9},{9,1},{17,25},{25,17},{2,10},{10... | collective-permute-start | bytes 3080 | tf_op jit(solution)/shard_map/ppermute | solution.py:59
  443.7 30.9 %collective-permute-start.133 = (bf16[1,512]{1,0:T(2,128)(2,1)}, bf16[1,512]{1,0:T(2,128)(2,1)}, u32[]{:S(2)}, u32[]{:S(2)}) collective-permute-start(bf16[1,512]{1,0:T(2,128)(2,1)} %get-tuple-element.83), channel_id=1, source_target_pairs={{0,16},{8,24},{16,0},{24,8},{1,17},{9,25},{17,1},{25,9},{2,18},{10... | collective-permute-start | bytes 3080 | tf_op jit(solution)/shard_map/ppermute | solution.py:59
  443.7 31.5 %collective-permute-start.134 = (bf16[1,512]{1,0:T(2,128)(2,1)}, bf16[1,512]{1,0:T(2,128)(2,1)}, u32[]{:S(2)}, u32[]{:S(2)}) collective-permute-start(bf16[1,512]{1,0:T(2,128)(2,1)} %get-tuple-element.83), channel_id=1, source_target_pairs={{0,24},{8,16},{16,8},{24,0},{1,25},{9,17},{17,9},{25,1},{2,26},{10... | collective-permute-start | bytes 3080 | tf_op jit(solution)/shard_map/ppermute | solution.py:59
  474.6 57.4 %collective-permute-start.94 = (bf16[1,256,2048]{2,1,0:T(8,128)(2,1)}, bf16[1,256,2048]{2,1,0:T(8,128)(2,1)}, u32[]{:S(2)}, u32[]{:S(2)}) collective-permute-start(bf16[1,256,2048]{2,1,0:T(8,128)(2,1)} %collective-permute-done.93), channel_id=1, source_target_pairs={{0,4},{4,0},{1,5},{5,1},{2,6},{6,2},{3,7},{7,3},{8,12},{12,8},{9,1... | collective-permute-start | bytes 3145736 | tf_op jit(solution)/shard_map/ppermute | solution.py:62
  475.2 15.4 %collective-permute-start.27 = (bf16[144,1024]{1,0:T(8,128)(2,1)S(1)}, bf16[144,1024]{1,0:T(8,128)(2,1)}, u32[]{:S(2)}, u32[]{:S(2)}) collective-permute-start(bf16[144,1024]{1,0:T(8,128)(2,1)S(1)} %get-tuple-element.57), channel_id=1, source_target_pairs={{0,16},{8,24},{16,0},{24,8},{1,17},{9,25},{17,1},{25,9},{2,18},{10... | collective-permute-start | bytes 884744 | tf_op jit(solution)/shard_map/ppermute | solution.py:59
  486.6 14.5 %collective-permute-start.29 = (bf16[144,1024]{1,0:T(8,128)(2,1)S(1)}, bf16[144,1024]{1,0:T(8,128)(2,1)S(1)}, u32[]{:S(2)}, u32[]{:S(2)}) collective-permute-start(bf16[144,1024]{1,0:T(8,128)(2,1)S(1)} %fusion.129), channel_id=1, source_target_pairs={{0,8},{8,0},{16,24},{24,16},{1,9},{9,1},{17,25},{25,17},{2,10},{10... | collective-permute-start | bytes 884744 | tf_op jit(solution)/shard_map/ppermute | solution.py:59
  490.6 19.0 %collective-permute-start.30 = (bf16[144,1024]{1,0:T(8,128)(2,1)}, bf16[144,1024]{1,0:T(8,128)(2,1)}, u32[]{:S(2)}, u32[]{:S(2)}) collective-permute-start(bf16[144,1024]{1,0:T(8,128)(2,1)} %get-tuple-element.59), channel_id=1, source_target_pairs={{0,8},{8,0},{16,24},{24,16},{1,9},{9,1},{17,25},{25,17},{2,10},{10... | collective-permute-start | bytes 884744 | tf_op jit(solution)/shard_map/ppermute | solution.py:59
  514.9 21.5 %collective-permute-start.113 = (f32[2048]{0:T(1024)}, f32[2048]{0:T(1024)S(1)}, u32[]{:S(2)}, u32[]{:S(2)}) collective-permute-start(f32[2048]{0:T(1024)} %bitcast.204), channel_id=1, source_target_pairs={{0,8},{8,0},{16,24},{24,16},{1,9},{9,1},{17,25},{25,17},{2,10},{10... | collective-permute-start | bytes 24584 | tf_op jit(solution)/shard_map/ppermute | solution.py:59
  515.4 21.6 %collective-permute-start.114 = (f32[2048]{0:T(1024)}, f32[2048]{0:T(1024)}, u32[]{:S(2)}, u32[]{:S(2)}) collective-permute-start(f32[2048]{0:T(1024)} %bitcast.204), channel_id=1, source_target_pairs={{0,16},{8,24},{16,0},{24,8},{1,17},{9,25},{17,1},{25,9},{2,18},{10... | collective-permute-start | bytes 24584 | tf_op jit(solution)/shard_map/ppermute | solution.py:59
  534.3 15.5 %collective-permute-start.47 = (bf16[144,1024]{1,0:T(8,128)(2,1)S(1)}, bf16[144,1024]{1,0:T(8,128)(2,1)}, u32[]{:S(2)}, u32[]{:S(2)}) collective-permute-start(bf16[144,1024]{1,0:T(8,128)(2,1)S(1)} %copy-done.33), channel_id=1, source_target_pairs={{0,16},{8,24},{16,0},{24,8},{1,17},{9,25},{17,1},{25,9},{2,18},{10... | collective-permute-start | bytes 884744 | tf_op jit(solution)/shard_map/ppermute | solution.py:59
  547.0 43.1 %collective-permute-start.87 = (bf16[4,64,2048]{2,1,0:T(8,128)(2,1)}, bf16[4,64,2048]{2,1,0:T(8,128)(2,1)}, u32[]{:S(2)}, u32[]{:S(2)}) collective-permute-start(bf16[4,64,2048]{2,1,0:T(8,128)(2,1)} %collective-permute-done.86), channel_id=1, source_target_pairs={{0,4},{4,0},{1,5},{5,1},{2,6},{6,2},{3,7},{7,3},{8,12},{12,8},{9,1... | collective-permute-start | bytes 3145736 | tf_op jit(solution)/shard_map/ppermute | solution.py:62
  592.5 16.8 %collective-permute-start.72 = (bf16[144,1024]{1,0:T(8,128)(2,1)}, bf16[144,1024]{1,0:T(8,128)(2,1)}, u32[]{:S(2)}, u32[]{:S(2)}) collective-permute-start(bf16[144,1024]{1,0:T(8,128)(2,1)} %get-tuple-element.55), channel_id=1, source_target_pairs={{0,8},{8,0},{16,24},{24,16},{1,9},{9,1},{17,25},{25,17},{2,10},{10... | collective-permute-start | bytes 884744 | tf_op jit(solution)/shard_map/ppermute | solution.py:59
  617.2 23.0 %collective-permute-start.104 = (f32[2048]{0:T(1024)}, f32[2048]{0:T(1024)S(1)}, u32[]{:S(2)}, u32[]{:S(2)}) collective-permute-start(f32[2048]{0:T(1024)} %bitcast.186), channel_id=1, source_target_pairs={{0,8},{8,0},{16,24},{24,16},{1,9},{9,1},{17,25},{25,17},{2,10},{10... | collective-permute-start | bytes 24584 | tf_op jit(solution)/shard_map/ppermute | solution.py:59
  618.2 23.1 %collective-permute-start.105 = (f32[2048]{0:T(1024)}, f32[2048]{0:T(1024)}, u32[]{:S(2)}, u32[]{:S(2)}) collective-permute-start(f32[2048]{0:T(1024)} %bitcast.186), channel_id=1, source_target_pairs={{0,16},{8,24},{16,0},{24,8},{1,17},{9,25},{17,1},{25,9},{2,18},{10... | collective-permute-start | bytes 24584 | tf_op jit(solution)/shard_map/ppermute | solution.py:59
  619.9 23.5 %collective-permute-start.106 = (f32[2048]{0:T(1024)}, f32[2048]{0:T(1024)}, u32[]{:S(2)}, u32[]{:S(2)}) collective-permute-start(f32[2048]{0:T(1024)} %bitcast.186), channel_id=1, source_target_pairs={{0,24},{8,16},{16,8},{24,0},{1,25},{9,17},{17,9},{25,1},{2,26},{10... | collective-permute-start | bytes 24584 | tf_op jit(solution)/shard_map/ppermute | solution.py:59
  640.1 47.8 %collective-permute-start.101 = (f32[1,2048]{1,0:T(1,128)S(1)}, f32[1,2048]{1,0:T(1,128)}, u32[]{:S(2)}, u32[]{:S(2)}) collective-permute-start(f32[1,2048]{1,0:T(1,128)S(1)} %bitcast.914), channel_id=1, source_target_pairs={{0,8},{8,0},{16,24},{24,16},{1,9},{9,1},{17,25},{25,17},{2,10},{10... | collective-permute-start | bytes 24584 | tf_op jit(solution)/shard_map/ppermute | solution.py:59
  652.0 37.0 %collective-permute-start.102 = (f32[1,2048]{1,0:T(1,128)S(1)}, f32[1,2048]{1,0:T(1,128)S(1)}, u32[]{:S(2)}, u32[]{:S(2)}) collective-permute-start(f32[1,2048]{1,0:T(1,128)S(1)} %bitcast.915), channel_id=1, source_target_pairs={{0,16},{8,24},{16,0},{24,8},{1,17},{9,25},{17,1},{25,9},{2,18},{10... | collective-permute-start | bytes 24584 | tf_op jit(solution)/shard_map/ppermute | solution.py:59
  653.7 36.6 %collective-permute-start.103 = (f32[1,2048]{1,0:T(1,128)S(1)}, f32[1,2048]{1,0:T(1,128)S(1)}, u32[]{:S(2)}, u32[]{:S(2)}) collective-permute-start(f32[1,2048]{1,0:T(1,128)S(1)} %bitcast.916), channel_id=1, source_target_pairs={{0,24},{8,16},{16,8},{24,0},{1,25},{9,17},{17,9},{25,1},{2,26},{10... | collective-permute-start | bytes 24584 | tf_op jit(solution)/shard_map/ppermute | solution.py:59
  671.8 20.6 %collective-permute-start.112 = (f32[4,2048]{1,0:T(4,128)S(1)}, f32[4,2048]{1,0:T(4,128)S(1)}, u32[]{:S(2)}, u32[]{:S(2)}) collective-permute-start(f32[4,2048]{1,0:T(4,128)S(1)} %fusion.368), channel_id=1, source_target_pairs={{0,24},{8,16},{16,8},{24,0},{1,25},{9,17},{17,9},{25,1},{2,26},{10... | collective-permute-start | bytes 98312 | tf_op jit(solution)/shard_map/ppermute | solution.py:59
  673.5 18.9 %collective-permute-start.111 = (f32[4,2048]{1,0:T(4,128)S(1)}, f32[4,2048]{1,0:T(4,128)S(1)}, u32[]{:S(2)}, u32[]{:S(2)}) collective-permute-start(f32[4,2048]{1,0:T(4,128)S(1)} %fusion.368), channel_id=1, source_target_pairs={{0,16},{8,24},{16,0},{24,8},{1,17},{9,25},{17,1},{25,9},{2,18},{10... | collective-permute-start | bytes 98312 | tf_op jit(solution)/shard_map/ppermute | solution.py:59
  689.0 92.0 %collective-permute-start.96 = (bf16[144,1024]{1,0:T(8,128)(2,1)}, bf16[144,1024]{1,0:T(8,128)(2,1)}, u32[]{:S(2)}, u32[]{:S(2)}) collective-permute-start(bf16[144,1024]{1,0:T(8,128)(2,1)} %get-tuple-element.50), channel_id=1, source_target_pairs={{0,16},{8,24},{16,0},{24,8},{1,17},{9,25},{17,1},{25,9},{2,18},{10... | collective-permute-start | bytes 884744 | tf_op jit(solution)/shard_map/ppermute | solution.py:59
  690.3 141.6 %collective-permute-start.95 = (bf16[144,1024]{1,0:T(8,128)(2,1)}, bf16[144,1024]{1,0:T(8,128)(2,1)}, u32[]{:S(2)}, u32[]{:S(2)}) collective-permute-start(bf16[144,1024]{1,0:T(8,128)(2,1)} %get-tuple-element.47), channel_id=1, source_target_pairs={{0,16},{8,24},{16,0},{24,8},{1,17},{9,25},{17,1},{25,9},{2,18},{10... | collective-permute-start | bytes 884744 | tf_op jit(solution)/shard_map/ppermute | solution.py:59
  744.1 38.9 %all-to-all-start.6 = ((bf16[32,2,1088]{2,1,0:T(2,128)(2,1)}), bf16[32,2,1088]{2,1,0:T(2,128)(2,1)}, u32[]{:S(2)}, u32[]{:S(2)}) async-start(bf16[32,2,1088]{2,1,0:T(2,128)(2,1)} %reshape.1847), calls=%async_computation.6 | async-start | bytes 294912 | tf_op jit(solution)/shard_map/all_to_all | solution.py:361
  754.2 77.7 %collective-permute-start.99 = (bf16[144,1024]{1,0:T(8,128)(2,1)}, bf16[144,1024]{1,0:T(8,128)(2,1)}, u32[]{:S(2)}, u32[]{:S(2)}) collective-permute-start(bf16[144,1024]{1,0:T(8,128)(2,1)} %get-tuple-element.48), channel_id=1, source_target_pairs={{0,8},{8,0},{16,24},{24,16},{1,9},{9,1},{17,25},{25,17},{2,10},{10... | collective-permute-start | bytes 884744 | tf_op jit(solution)/shard_map/ppermute | solution.py:59
  756.5 83.4 %collective-permute-start.98 = (bf16[144,1024]{1,0:T(8,128)(2,1)}, bf16[144,1024]{1,0:T(8,128)(2,1)}, u32[]{:S(2)}, u32[]{:S(2)}) collective-permute-start(bf16[144,1024]{1,0:T(8,128)(2,1)} %get-tuple-element.49), channel_id=1, source_target_pairs={{0,8},{8,0},{16,24},{24,16},{1,9},{9,1},{17,25},{25,17},{2,10},{10... | collective-permute-start | bytes 884744 | tf_op jit(solution)/shard_map/ppermute | solution.py:59
  780.5 17.6 %collective-permute-start.138 = (bf16[4,4,9216]{2,1,0:T(4,128)(2,1)S(1)}, bf16[4,4,9216]{2,1,0:T(4,128)(2,1)S(1)}, u32[]{:S(2)}, u32[]{:S(2)}) collective-permute-start(bf16[4,4,9216]{2,1,0:T(4,128)(2,1)S(1)} %pad_maximum_fusion.10), channel_id=1, source_target_pairs={{0,4},{4,0},{1,5},{5,1},{2,6},{6,2},{3,7},{7,3},{8,12},{12,8},{9,1... | collective-permute-start | bytes 884744 | tf_op jit(solution)/shard_map/ppermute | solution.py:62
  781.1 22.2 %collective-permute-start.129 = (bf16[8,4,4608]{2,1,0:T(4,128)(2,1)S(1)}, bf16[8,4,4608]{2,1,0:T(4,128)(2,1)S(1)}, u32[]{:S(2)}, u32[]{:S(2)}) collective-permute-start(bf16[8,4,4608]{2,1,0:T(4,128)(2,1)S(1)} %constant_dynamic-update-slice_fusion.21), channel_id=1, source_target_pairs={{0,8},{8,0},{16,24},{24,16},{1,9},{9,1},{17,25},{25,17},{2,10},{10... | collective-permute-start | bytes 884744 | tf_op jit(solution)/shard_map/ppermute | solution.py:59
  809.6 22.3 %collective-permute-start.97 = (bf16[144,1024]{1,0:T(8,128)(2,1)}, bf16[144,1024]{1,0:T(8,128)(2,1)}, u32[]{:S(2)}, u32[]{:S(2)}) collective-permute-start(bf16[144,1024]{1,0:T(8,128)(2,1)} %fusion.113), channel_id=1, source_target_pairs={{0,8},{8,0},{16,24},{24,16},{1,9},{9,1},{17,25},{25,17},{2,10},{10... | collective-permute-start | bytes 884744 | tf_op jit(solution)/shard_map/ppermute | solution.py:59
  (213 other events, 1762.8 us)

commit v2 on v1

--- a/solution.py
+++ b/solution.py
@@ -40,7 +40,8 @@
     bit = 1
     while bit < size:
         split = stack.reshape((size // (2 * bit), 2, bit) + stack.shape[1:])
-        stack = jnp.where((me & bit) != 0, split[:, ::-1], split).reshape(stack.shape)
+        turned = jnp.concatenate([split[:, 1:], split[:, :1]], axis=1)
+        stack = jnp.where((me & bit) != 0, turned, split).reshape(stack.shape)
         bit *= 2
     return stack
 
@@ -64,32 +65,15 @@
     def other_plane(self, value, k):
         return lax.ppermute(value, "fsdp", [(i, i ^ k) for i in range(self.planes)])
 
-    def spread(self, value, bits):
-        held = {0: value}
-        for bit in bits:
-            held.update({j | bit: self.hop(v, bit) for j, v in list(held.items())})
-        return [held[j] for j in range(self.tp)]
-
-    def gather_tp(self, halves):
-        bits = bits_of(self.tp)
-        left, right = self.spread(halves[0], bits), self.spread(halves[1], bits[::-1])
-        return left, right
-
-    def collect(self, parts, bits):
-        held = dict(enumerate(parts))
-        for bit in bits[::-1]:
-            for j in [j for j in held if not j & bit]:
-                came = self.hop(held[j | bit].astype(BF), bit)
-                held[j] = held[j] + came.astype(F32)
-                del held[j | bit]
-        return held[0]
-
-    def scatter_tp(self, partial):
-        half = partial.shape[2] // 2
-        bits = bits_of(self.tp)
-        left = self.collect([partial[j, :, :half] for j in range(self.tp)], bits)
-        right = self.collect([partial[j, :, half:] for j in range(self.tp)], bits[::-1])
-        return jnp.concatenate([left, right], axis=1)
+    def spread(self, value):
+        return [value] + [self.hop(value, j) for j in range(1, self.tp)]
+
+    def collect(self, partial):
+        total = partial[0]
+        low = partial.astype(BF)
+        for j in range(1, self.tp):
+            total = total + self.hop(low[j], j).astype(F32)
+        return total
 
     def tp_direct(self, value):
         return jnp.stack([value] + [self.hop(value, j) for j in range(1, self.tp)])
@@ -109,54 +93,17 @@
         return jnp.concatenate([planes, self.other_core(planes)])
 
 
-    def swap_halves(self, value):
-        half = value.shape[-1] // 2
-        turned = jnp.concatenate([value[..., half:], value[..., :half]], axis=-1)
-        return jnp.where(self.c == 0, value, turned)
-
-    def own_halves(self, value):
-        split = value.reshape(value.shape[:-1] + (self.tp, 2, -1))
-        first, second = split[..., 0, :], split[..., 1, :]
-        shape = value.shape[:-1] + (value.shape[-1] // 2,)
-        return (
-            jnp.where(self.c == 0, first, second).reshape(shape),
-            jnp.where(self.c == 0, second, first).reshape(shape),
-        )
-
-    def natural(self, value):
-        split = value.reshape(value.shape[:-1] + (2, self.tp, -1))
-        first, second = split[..., 0, :, :], split[..., 1, :, :]
-        both = jnp.stack(
-            [jnp.where(self.c == 0, first, second), jnp.where(self.c == 0, second, first)], axis=-2
-        )
-        return both.reshape(value.shape)
-
-
-    def rings(self, block):
-        lead, rows, n = block.shape
-        held = jnp.zeros((2, lead, self.planes, rows, n), block.dtype)
-        for k in range(self.planes):
-            if k:
-                block = lax.ppermute(
-                    block, "fsdp", [(i, (i + 1) % self.planes) for i in range(self.planes)]
-                )
-            at = lax.rem(self.z + self.planes - k, self.planes)
-            held = lax.dynamic_update_slice(held, block[None, :, None], (0, 0, at, 0, 0))
-            held = lax.dynamic_update_slice(
-                held, self.other_core(block)[None, :, None], (1, 0, at, 0, 0)
-            )
-        return held
-
     def shuffle(self, shard, blocks):
         rows = shard.shape[0]
         split = shard.reshape(rows, blocks, self.tp, -1).transpose(2, 0, 1, 3)
         return lax.all_to_all(split.reshape(self.tp, rows, -1), "tp", 0, 0, tiled=True)
 
     def by_columns(self, shuffled):
-        return self.rings(shuffled).reshape(-1, shuffled.shape[2])
+        whole = lax.all_gather(shuffled, ("core", "fsdp"), axis=1, tiled=True)
+        return whole.reshape(-1, shuffled.shape[2])
 
     def by_rows(self, shard):
-        return self.rings(shard[None]).reshape(-1, shard.shape[1])
+        return lax.all_gather(shard, ("core", "fsdp"), axis=0, tiled=True)
 
 
 def attend(queries, key_heads, value_heads, bias):
@@ -214,13 +161,13 @@
     own = width // world
     scale = HDIM ** (-0.5)
 
-    qkv_rel = me.by_columns(me.shuffle(w_qkv, 3))
-    out_rel = me.by_rows(w_attn_out)
-    kv_rel = me.by_columns(me.shuffle(w_cross_kv, 2))
-    cq_rel = me.by_columns(me.shuffle(w_cross_q, 1))
-    cout_rel = me.by_rows(w_cross_out)
-    up_rel = me.by_columns(me.shuffle(w_up, 1))
-    down_rel = me.by_rows(w_down)
+    qkv = me.by_columns(me.shuffle(w_qkv, 3))
+    out_w = me.by_rows(w_attn_out)
+    kv = me.by_columns(me.shuffle(w_cross_kv, 2))
+    cq = me.by_columns(me.shuffle(w_cross_q, 1))
+    cout = me.by_rows(w_cross_out)
+    up = me.by_columns(me.shuffle(w_up, 1))
+    down = me.by_rows(w_down)
 
     vectors = jnp.stack([mask_embed, gain_attn, gain_cross, gain_mlp])
     vectors = me.tp_direct(me.gather_cz(vectors)).reshape(world, 4, own)
@@ -243,7 +190,7 @@
     start = jnp.concatenate([start_free, jnp.broadcast_to(embed[None], (PAD, width))])
 
     cot_sum = jnp.sum(cotangent[0].astype(F32), axis=0)
-    cot_all = lax.all_gather(cot_sum[None], ("core", "fsdp"), axis=0, tiled=True)
+    cot_all = xor_order(me.gather_cz(cot_sum), me.c * planes + me.z, 2 * planes)
     cot_group = me.tp_direct(cot_sum[None])[:, 0]
     cot_high = cot_group.astype(BF)
 
@@ -257,25 +204,14 @@
     through = lax.all_to_all(through, ("core", "fsdp"), 0, 0, tiled=True)
     grad_active = through.transpose(1, 0, 2).reshape(tp, -1)
 
-    text_left, text_right = me.gather_tp(me.own_halves(text[0]))
-    text_rows = jnp.concatenate(
-        [jnp.concatenate(text_left), jnp.concatenate(text_right)], axis=1
-    )
+    text_rows = jnp.concatenate(me.spread(text[0]))
     open_text = lax.broadcasted_iota(jnp.int32, (1, txt), 1) < text_lengths[:, None]
     text_bias = jnp.where(me.tp_direct(open_text.astype(F32))[:, 0] > 0, 0.0, -1e30)
 
     field_a, scale_a = normed(start)
     entries = (field_a * gain_a[None]).astype(BF)
-    ent_left, ent_right = me.own_halves(entries)
-    got_left, got_right = me.gather_tp((ent_left[:free], ent_right[:free]))
-    ent_rows = jnp.concatenate(
-        [
-            jnp.concatenate(got_left + [ent_left[free:]]),
-            jnp.concatenate(got_right + [ent_right[free:]]),
-        ],
-        axis=1,
-    )
-    packed = dot(ent_rows, qkv_rel).astype(BF)
+    ent_rows = jnp.concatenate(me.spread(entries[:free]) + [entries[free:]])
+    packed = dot(ent_rows, qkv).astype(BF)
     packed_free = packed[: tp * free].reshape(tp, free, 3, local, HDIM)
     packed_masked = packed[tp * free :].reshape(1, PAD, 3, local, HDIM)
     packed = jnp.concatenate(
@@ -288,29 +224,27 @@
     )
     probs, mixture = attend(queries, key_heads, value_heads, key_bias)
     mixture = mixture.reshape(tp, rows, local * HDIM)
-    added = dot(me.swap_halves(mixture).reshape(tp * rows, -1), out_rel)
-    after_attn = start + me.scatter_tp(added.reshape(tp, rows, width))
+    added = dot(mixture.reshape(tp * rows, -1), out_w)
+    after_attn = start + me.collect(added.reshape(tp, rows, width))
 
     field_c, scale_c = normed(after_attn)
     cross_entries = (field_c * gain_c[None]).astype(BF)
-    got_left, got_right = me.gather_tp(me.own_halves(cross_entries))
-    cross_rows = jnp.concatenate([jnp.concatenate(got_left), jnp.concatenate(got_right)], axis=1)
-    cross_queries = dot(cross_rows, cq_rel).astype(BF).reshape(tp, rows, local, HDIM)
-    pair = dot(text_rows, kv_rel).astype(BF).reshape(tp, txt, 2, local, HDIM)
+    cross_rows = jnp.concatenate(me.spread(cross_entries))
+    cross_queries = dot(cross_rows, cq).astype(BF).reshape(tp, rows, local, HDIM)
+    pair = dot(text_rows, kv).astype(BF).reshape(tp, txt, 2, local, HDIM)
     text_keys, text_values = pair[:, :, 0], pair[:, :, 1]
     cross_probs, cross_mix = attend(cross_queries, text_keys, text_values, text_bias)
     cross_mix = cross_mix.reshape(tp, rows, local * HDIM)
-    added = dot(me.swap_halves(cross_mix).reshape(tp * rows, -1), cout_rel)
-    after_cross = after_attn + me.scatter_tp(added.reshape(tp, rows, width))
+    added = dot(cross_mix.reshape(tp * rows, -1), cout)
+    after_cross = after_attn + me.collect(added.reshape(tp, rows, width))
 
     field_m, scale_m = normed(after_cross)
     mlp_entries = (field_m * gain_m[None]).astype(BF)
-    got_left, got_right = me.gather_tp(me.own_halves(mlp_entries))
-    mlp_rows = jnp.concatenate([jnp.concatenate(got_left), jnp.concatenate(got_right)], axis=1)
-    hidden = dot(mlp_rows, up_rel)
+    mlp_rows = jnp.concatenate(me.spread(mlp_entries))
+    hidden = dot(mlp_rows, up)
     active = jax.nn.gelu(hidden).astype(BF)
-    added = dot(me.swap_halves(active), down_rel)
-    output = after_cross + me.scatter_tp(added.reshape(tp, rows, width))
+    added = dot(active, down)
+    output = after_cross + me.collect(added.reshape(tp, rows, width))
     output = dot(place, output.astype(BF)).astype(BF)
 
     field_c1, scale_c1 = normed(me.tp_direct(after_attn[free]))
@@ -320,12 +254,12 @@
     active_one, gelu_back = jax.vjp(jax.nn.gelu, hidden_one)
     active_one = active_one.astype(BF)
     grad_pre = gelu_back(grad_active)[0].astype(BF)
-    grad_entry = me.natural(me.tp_sum(dot_t(grad_pre, up_rel)))
+    grad_entry = me.tp_sum(dot_t(grad_pre, up))
     grad_gain_m = grad_entry[0] * field_m1[0]
     grad_mid = cot_group + norm_back(grad_entry * gain_m[None], field_m1, scale_m1)
     low_mid = grad_mid.astype(BF)
 
-    grad_cmix = me.swap_halves(dot_t(low_mid, cout_rel)).astype(BF)
+    grad_cmix = dot_t(low_mid, cout).astype(BF)
     query_one = cross_queries[:, free]
     cross_probs_one = cross_probs[:, :, free]
     grad_scores, grad_cq = attend_back(
@@ -333,7 +267,7 @@
     )
     grad_cq = grad_cq.reshape(tp, -1).astype(BF)
     query_one = query_one.reshape(tp, -1)
-    grad_entry = me.natural(me.tp_sum(dot_t(grad_cq, cq_rel)))
+    grad_entry = me.tp_sum(dot_t(grad_cq, cq))
     grad_gain_c = grad_entry[0] * field_c1[0]
     grad_attn = grad_mid + norm_back(grad_entry * gain_c[None], field_c1, scale_c1)
     low_attn = grad_attn.astype(BF)
@@ -344,13 +278,13 @@
             jnp.pad(head_blocks(grad_cmix, local), ((0, 0), (local * HDIM, 0))),
         ]
     )
-    rows_back = dot_t(heads_back, kv_rel).reshape(2, tp, local, width)
+    rows_back = dot_t(heads_back, kv).reshape(2, tp, local, width)
     rows_back = jnp.stack([rows_back[0] * scale, rows_back[1]], axis=1).astype(BF)
     weighs = jnp.stack([grad_scores, cross_probs_one.astype(BF)], axis=1)
     sent = jnp.concatenate([rows_back, weighs], axis=-1).reshape(tp, 2 * local, width + txt)
     sent = me.to_owner(sent)
     weighs = sent[:, :, width:].reshape(tp * 2 * local, txt)
-    rows_back = me.natural(sent[:, :, :width].reshape(tp * 2 * local, width))
+    rows_back = sent[:, :, :width].reshape(tp * 2 * local, width)
     grad_text = dot_sum(weighs, rows_back).astype(BF)
     weighs = xor_order(sent[:, :, width:], me.t, tp).reshape(tp * 2 * local, txt)
     left_text = dot(weighs, text[0]).astype(BF)
@@ -360,7 +294,7 @@
     lefts = lefts.reshape(-1, world, own).transpose(1, 0, 2)
     lefts = lax.all_to_all(lefts, ("tp", "core", "fsdp"), 0, 0, tiled=True)
 
-    grad_amix = me.swap_halves(dot_t(low_attn, out_rel)).astype(BF)
+    grad_amix = dot_t(low_attn, out_w).astype(BF)
     attn_scores, grad_q = attend_back(
         queries[:, free],
         key_heads,
@@ -378,7 +312,7 @@
             jnp.pad(grad_q, ((0, 0), (0, 2 * span))),
         ]
     )
-    rows_back = dot_t(heads_back, qkv_rel)
+    rows_back = dot_t(heads_back, qkv)
     value_rows = rows_back[: tp * local].reshape(tp, local, width)
     key_rows = rows_back[tp * local : tp * local + local] * scale
     query_rows = rows_back[tp * local + local :].reshape(tp, 1, width)
@@ -391,7 +325,7 @@
     sent = me.to_owner(jnp.concatenate([rows_back, weighs], axis=-1))
     count = 2 * local + 1
     weighs = sent[:, :, width:].reshape(tp * count, rows)
-    rows_back = me.natural(sent[:, :, :width].reshape(tp * count, width))
+    rows_back = sent[:, :, :width].reshape(tp * count, width)
     grad_entry = dot_sum(weighs, rows_back)
     weighs = xor_order(sent[:, : 2 * local, width:], me.t, tp).reshape(tp * 2 * local, rows)
     left_attn = dot(weighs, entries)

time: 857 us -> 556 us (0.65)
  local copies, waits for them, and re-layouts: 254 us -> 107 us
  waiting for transfers between devices: 241 us -> 147 us
  starting transfers between devices: 146 us -> 101 us
  other arithmetic: 78.1 us -> 40 us
  blocking collectives: 26.1 us -> 46.2 us
  between operations: 4.68 us -> 17.6 us
    ppermute x21 -> x0, waiting for transfers between devices: 160 us -> none  [rings(): lax.ppermute(block, 'fsdp', [(i, (i + 1) % self.planes) for i in range(se...]
    dynamic_update_slice x56 -> x0, local copies, waits for them, and re-layouts: 77.2 us -> none  [the longest x28 39.2 us: rings(): lax.dynamic_update_slice(held, block[None, :, None], (0, 0, at, 0, 0))]
    all_to_all x0 -> x4, blocking collectives: none -> 46.2 us  [shuffle(): lax.all_to_all(split.reshape(self.tp, rows, -1), 'tp', 0, 0, tiled=True)]
    all_gather x0 -> x7, waiting for transfers between devices: none -> 44.3 us  [the longest x3 38.3 us: by_rows(): return lax.all_gather(shard, ('core', 'fsdp'), axis=0, tiled=True)]
    ppermute x78 -> x57, waiting for transfers between devices: 56.2 us -> 95.2 us  [hop(): return lax.ppermute(value, 'tp', [(i, i ^ j) for i in range(self.tp)])]
    concatenate x20 -> x23, local copies, waits for them, and re-layouts: 30.6 us -> 2.13 us  [the longest x22 1.51 us: xor_order(): turned = jnp.concatenate([split[:, 1:], split[:, :1]], axis=1)]
    all_gather x1 -> x0, blocking collectives: 26.1 us -> none  [shards(): lax.all_gather(cot_sum[None], ('core', 'fsdp'), axis=0, tiled=True)]
    ppermute x78 -> x57, starting transfers between devices: 90.7 us -> 67.4 us  [hop(): return lax.ppermute(value, 'tp', [(i, i ^ j) for i in range(self.tp)])]
  transfers between devices with their start and end apart: 146 -> 83, of which waited for: 47 -> 22; matrix products, arithmetic and copies ran while one was open for 48% -> 41% of each run, Pallas kernels for 0% -> 0%
where the time goes in v2:
time: 556 us; the launch traced here: 548 us
  waiting for transfers between devices  147 us (26%)
  local copies, waits for them, and re-layouts  107 us (19%)
  starting transfers between devices  101 us (18%)
  matrix products  88.8 us (16%)
  blocking collectives  46.2 us (8%)
  other arithmetic  40 us (7%)
  between operations  17.6 us (3%)
    ppermute x57, waiting for transfers between devices, hop(): return lax.ppermute(value, 'tp', [(i, i ^ j) for i in range(self.tp)])  95.2 us
    ppermute x57, starting transfers between devices, hop(): return lax.ppermute(value, 'tp', [(i, i ^ j) for i in range(self.tp)])  67.4 us
    dot_general x13, matrix products, dot(): return jnp.dot(left, right, preferred_element_type=F32)  51.8 us
    all_to_all x4, blocking collectives, shuffle(): lax.all_to_all(split.reshape(self.tp, rows, -1), 'tp', 0, 0, tiled=True)  46.2 us
    all_gather x3, waiting for transfers between devices, by_rows(): return lax.all_gather(shard, ('core', 'fsdp'), axis=0, tiled=True)  38.3 us
    unnamed x185, local copies, waits for them, and re-layouts  28.7 us
    ppermute x12, starting transfers between devices, other_plane(): return lax.ppermute(value, 'fsdp', [(i, i ^ k) for i in range(self.planes)])  21.1 us
    dot_general x7, matrix products, dot_t(): lax.dot_general(left, right, (((1,), (1,)), ((), ())), preferred_element_...  15.8 us
  transfers between devices with their start and end apart: 83, of which 22 were waited for; matrix products, arithmetic and copies ran while one was open for 41% of the time, Pallas kernels for 0%

profile of v2, /device:TPU:0, one launch (start us, length us, event | category | flops | bytes accessed | tf_op | source)
XLA Modules:
  0.0 548.4 jit_solution(4460163283831973044)
XLA Ops:
  8.6 10.7 %all_to_all.35 = bf16[4,64,512]{2,1,0:T(8,128)(2,1)S(1)} all-to-all(bf16[4,64,512]{2,1,0:T(8,128)(2,1)S(1)} %copy.638), channel_id=1, replica_groups=mesh['tp'=4,'core'=2,'fsdp'=4] {'tp'}, dimensions={0} | all-to-all | bytes 524288 | tf_op jit(solution)/shard_map/all_to_all | solution.py:99
  21.4 10.6 %all_to_all.36 = bf16[4,64,1024]{2,1,0:T(8,128)(2,1)} all-to-all(bf16[4,64,1024]{2,1,0:T(8,128)(2,1)S(1)} %reshape.1304), channel_id=1, replica_groups=mesh['tp'=4,'core'=2,'fsdp'=4] {'tp'}, dimensions={0} | all-to-all | bytes 1048576 | tf_op jit(solution)/shard_map/all_to_all | solution.py:99
  32.1 2.3 reshape.1299
  35.9 12.1 %all_to_all.37 = bf16[4,64,1536]{2,1,0:T(8,128)(2,1)} all-to-all(bf16[4,64,1536]{2,1,0:T(8,128)(2,1)S(1)} %reshape.1300), channel_id=1, replica_groups=mesh['tp'=4,'core'=2,'fsdp'=4] {'tp'}, dimensions={0} | all-to-all | bytes 1572864 | tf_op jit(solution)/shard_map/all_to_all | solution.py:99
  50.6 12.9 %all_to_all.38 = bf16[4,64,2048]{2,1,0:T(8,128)(2,1)S(1)} all-to-all(bf16[4,64,2048]{2,1,0:T(8,128)(2,1)S(1)} %copy.644), channel_id=1, replica_groups=mesh['tp'=4,'core'=2,'fsdp'=4] {'tp'}, dimensions={0} | all-to-all | bytes 2097152 | tf_op jit(solution)/shard_map/all_to_all | solution.py:99
  63.5 1.8 copy.645
  67.1 2.8 collective-permute-start.1
  86.1 3.7 collective-permute-start.38
  89.9 2.5 collective-permute-start.39
  104.3 1.8 collective-permute-start.8
  108.3 3.9 all-to-all-start.4
  113.0 2.2 copy.725
  115.2 3.5 all-to-all-done.4
  118.7 2.4 collective-permute-start.15
  121.1 1.9 constant_dynamic-update-slice_fusion.8
  123.0 17.2 %collective-permute-done.8 = bf16[128,2048]{1,0:T(8,128)(2,1)} collective-permute-done((bf16[128,2048]{1,0:T(8,128)(2,1)}, bf16[128,2048]{1,0:T(8,128)(2,1)}, u32[]{:S(2)}, u32[]{:S(2)}) %collective-permute-start.8) | collective-permute-done | bytes 524320 | tf_op jit(solution)/shard_map/ppermute | solution.py:60
  140.2 1.9 constant_dynamic-update-slice_fusion.7
  142.2 1.9 constant_dynamic-update-slice_fusion.6
  144.7 3.3 copy.640
  148.8 5.2 fusion.46
  155.5 2.4 fusion.283
  157.9 6.0 %all-gather.8.cloned.1.call-done = bf16[4,512,1536]{2,1,0:T(8,128)(2,1)} async-done(((bf16[4,64,1536]{2,1,0:T(8,128)(2,1)}), bf16[4,512,1536]{2,1,0:T(8,128)(2,1)}) %all-gather.8.cloned.1.call-update) | async-done | bytes 6291472 | tf_op jit(solution)/shard_map/all_gather | solution.py:102
  163.9 6.9 %convolution_convert_fusion = bf16[528,1536]{1,0:T(8,128)(2,1)S(1)} fusion(bf16[528,2048]{1,0:T(8,128)(2,1)} %constant_dynamic-update-slice_fusion.5, bf16[2048,1536]{1,0:T(8,128)(2,1)} %bitcast.645), kind=kOutput, calls=%fused_computation.13 | convolution fusion | flops 3322699776 | bytes 10076160 | tf_op jit(solution)/shard_map/dot_general | solution.py:14
  172.6 4.4 reshape.1302
  177.0 3.0 copy.634
  180.1 3.6 fusion.321
  183.7 2.2 broadcast_divide_fusion
  193.1 5.2 fusion.324
  205.6 10.4 %collective-permute-done.10 = bf16[144,2048]{1,0:T(8,128)(2,1)} collective-permute-done((bf16[144,2048]{1,0:T(8,128)(2,1)}, bf16[144,2048]{1,0:T(8,128)(2,1)}, u32[]{:S(2)}, u32[]{:S(2)}) %collective-permute-start.10) | collective-permute-done | bytes 589856 | tf_op jit(solution)/shard_map/ppermute | solution.py:60
  216.0 13.1 %collective-permute-done.11 = bf16[144,2048]{1,0:T(8,128)(2,1)} collective-permute-done((bf16[144,2048]{1,0:T(8,128)(2,1)}, bf16[144,2048]{1,0:T(8,128)(2,1)}, u32[]{:S(2)}, u32[]{:S(2)}) %collective-permute-start.11) | collective-permute-done | bytes 589856 | tf_op jit(solution)/shard_map/ppermute | solution.py:60
  229.1 2.0 fusion.277
  237.5 21.4 %collective-permute-done.47 = f32[2048]{0:T(1024)S(1)} collective-permute-done((f32[2048]{0:T(1024)S(1)}, f32[2048]{0:T(1024)S(1)}, u32[]{:S(2)}, u32[]{:S(2)}) %collective-permute-start.47) | collective-permute-done | bytes 8224 | tf_op jit(solution)/shard_map/ppermute | solution.py:60
  261.6 1.9 collective-permute-done.49
  263.7 2.2 fusion.51
  265.9 1.8 reshape.1310
  267.7 2.9 fusion.325
  274.0 5.2 fusion.328
  286.6 10.4 %collective-permute-done.22 = bf16[144,2048]{1,0:T(8,128)(2,1)} collective-permute-done((bf16[144,2048]{1,0:T(8,128)(2,1)}, bf16[144,2048]{1,0:T(8,128)(2,1)}, u32[]{:S(2)}, u32[]{:S(2)}) %collective-permute-start.22) | collective-permute-done | bytes 589856 | tf_op jit(solution)/shard_map/ppermute | solution.py:60
  297.1 10.6 %collective-permute-done.23 = bf16[144,2048]{1,0:T(8,128)(2,1)} collective-permute-done((bf16[144,2048]{1,0:T(8,128)(2,1)}, bf16[144,2048]{1,0:T(8,128)(2,1)}, u32[]{:S(2)}, u32[]{:S(2)}) %collective-permute-start.23) | collective-permute-done | bytes 589856 | tf_op jit(solution)/shard_map/ppermute | solution.py:60
  307.7 2.6 fusion.275
  325.3 11.5 %copy.646 = bf16[4,512,2048]{2,1,0:T(8,128)(2,1)} copy(bf16[4,512,2048]{2,0,1:T(4,128)(2,1)} %all-gather.18.cloned.1.call-done) | data formatting | bytes 16777216 | tf_op jit(solution)/shard_map/all_gather | solution.py:102
  338.5 8.6 %fusion.23 = f32[576,2048]{1,0:T(8,128)S(1)} fusion(bf16[2048,2048]{1,0:T(8,128)(2,1)} %bitcast.621, bf16[144,2048]{1,0:T(8,128)(2,1)} %collective-permute-done.27, bf16[144,2048]{1,0:T(8,128)(2,1)} %collective-permute-done.26, bf16[144,2048]{1,0:T(8,128)(2,1)} %collective-permute-done.25, bf16[144,2048]{1,0:T(8,128)(2,1)S(1)} %multiply_convert_fusion), kind=kOutput, calls=%fused_computation.30 | convolution fusion | flops 4841275392 | bytes 15466496 | tf_op jit(solution)/shard_map/dot_general | solution.py:14
  347.2 2.3 fusion.333
  351.6 37.4 %all-gather.20.cloned.1.call-done = bf16[2048,2048]{1,0:T(8,128)(2,1)} async-done(((bf16[256,2048]{1,0:T(8,128)(2,1)}), bf16[2048,2048]{1,0:T(8,128)(2,1)}) %all-gather.20.cloned.1.call-update) | async-done | bytes 8388624 | tf_op jit(solution)/shard_map/all_gather | solution.py:106
  389.0 11.2 %fusion.329 = (bf16[576,2048]{1,0:T(8,128)(2,1)S(1)}, f32[576,2048]{1,0:T(8,128)}) fusion(bf16[2048,2048]{1,0:T(8,128)(2,1)} %all-gather.20.cloned.1.call-done, f32[576,2048]{1,0:T(8,128)} %copy-done.66), kind=kOutput, calls=%fused_computation.586 | convolution fusion | flops 4843634688 | bytes 20185088 | tf_op jit(solution)/shard_map/dot_general | solution.py:14
  402.1 2.4 collective-permute-start.46
  410.4 2.2 fusion.229
  412.7 1.9 collective-permute-start.50
  416.9 4.1 collective-permute-done.50
  422.7 2.2 constant_dynamic-update-slice_fusion.11
  425.1 3.5 fusion.149
  431.7 4.5 fusion.330
  446.2 3.0 collective-permute-start.61
  451.9 2.6 all-to-all-start.6
  464.9 1.7 collective-permute-start.69
  466.6 2.5 collective-permute-start.70
  477.6 1.9 pad_maximum_fusion.10
  487.1 4.9 all-to-all-start.5
  507.5 1.8 constant_dynamic-update-slice_fusion.31
  512.8 1.8 fusion.119
  515.3 1.9 fusion.286
  520.4 2.6 collective-permute-done.63
  528.6 1.8 fusion.210
  538.0 3.4 convolution_convert_fusion.2
  (652 shorter events, 186.2 us)
Async XLA Ops:
  7.2 137.5 %all-gather.14.cloned.1.call-start = ((), (), s32[]{:S(2)}) async-start(), calls=%async_computation.10 | async-start | bytes 2359296 | tf_op jit(solution)/shard_map/all_gather | solution.py:102
  20.2 127.8 %all-gather.12.cloned.1.call-start = ((), (), s32[]{:S(2)}) async-start(), calls=%async_computation.9 | async-start | bytes 4718592 | tf_op jit(solution)/shard_map/all_gather | solution.py:102
  32.0 131.9 %all-gather.8.cloned.1.call-start = ((), (), s32[]{:S(2)}) async-start(), calls=%async_computation.7 | async-start | bytes 7077888 | tf_op jit(solution)/shard_map/all_gather | solution.py:102
  48.0 145.1 %all-gather.10.cloned.1.call-start = ((), (), s32[]{:S(2)}) async-start(), calls=%async_computation.8 | async-start | bytes 2359296 | tf_op jit(solution)/shard_map/all_gather | solution.py:106
  48.6 225.4 %all-gather.16.cloned.1.call-start = ((), (), s32[]{:S(2)}) async-start(), calls=%async_computation.11 | async-start | bytes 2359296 | tf_op jit(solution)/shard_map/all_gather | solution.py:106
  49.2 276.1 %all-gather.18.cloned.1.call-start = ((), (), s32[]{:S(2)}) async-start(), calls=%async_computation.12 | async-start | bytes 9437184 | tf_op jit(solution)/shard_map/all_gather | solution.py:102
  65.4 323.6 %all-gather.20.cloned.1.call-start = ((), (), s32[]{:S(2)}) async-start(), calls=%async_computation.13 | async-start | bytes 9437184 | tf_op jit(solution)/shard_map/all_gather | solution.py:106
  65.7 10.3 %collective-permute-start = (bf16[4,64]{1,0:T(4,128)(2,1)S(1)}, bf16[4,64]{1,0:T(4,128)(2,1)S(1)}, u32[]{:S(2)}, u32[]{:S(2)}) collective-permute-start(bf16[4,64]{1,0:T(4,128)(2,1)S(1)} %get-tuple-element.38), channel_id=1, source_target_pairs={{0,1},{1,0},{2,3},{3,2},{4,5},{5,4},{6,7},{7,6},{8,9},{9,8},{10,11... | collective-permute-start | bytes 1544 | tf_op jit(solution)/shard_map/ppermute | solution.py:66
  67.1 10.3 %collective-permute-start.1 = (bf16[4,64]{1,0:T(4,128)(2,1)S(1)}, bf16[4,64]{1,0:T(4,128)(2,1)S(1)}, u32[]{:S(2)}, u32[]{:S(2)}) collective-permute-start(bf16[4,64]{1,0:T(4,128)(2,1)S(1)} %get-tuple-element.38), channel_id=1, source_target_pairs={{0,2},{1,3},{2,0},{3,1},{4,6},{5,7},{6,4},{7,5},{8,10},{9,11},{10,... | collective-permute-start | bytes 1544 | tf_op jit(solution)/shard_map/ppermute | solution.py:66
  69.9 8.6 %collective-permute-start.2 = (bf16[4,64]{1,0:T(4,128)(2,1)S(1)}, bf16[4,64]{1,0:T(4,128)(2,1)S(1)}, u32[]{:S(2)}, u32[]{:S(2)}) collective-permute-start(bf16[4,64]{1,0:T(4,128)(2,1)S(1)} %get-tuple-element.38), channel_id=1, source_target_pairs={{0,3},{1,2},{2,1},{3,0},{4,7},{5,6},{6,5},{7,4},{8,11},{9,10},{10,... | collective-permute-start | bytes 1544 | tf_op jit(solution)/shard_map/ppermute | solution.py:66
  70.1 77.9 %collective-permute-start.13 = (bf16[128,2048]{1,0:T(8,128)(2,1)}, bf16[128,2048]{1,0:T(8,128)(2,1)}, u32[]{:S(2)}, u32[]{:S(2)}) collective-permute-start(bf16[128,2048]{1,0:T(8,128)(2,1)} %bitcast.46), channel_id=1, source_target_pairs={{0,8},{8,0},{16,24},{24,16},{1,9},{9,1},{17,25},{25,17},{2,10},{10... | collective-permute-start | bytes 1572872 | tf_op jit(solution)/shard_map/ppermute | solution.py:60
  71.0 76.9 %collective-permute-start.14 = (bf16[128,2048]{1,0:T(8,128)(2,1)}, bf16[128,2048]{1,0:T(8,128)(2,1)}, u32[]{:S(2)}, u32[]{:S(2)}) collective-permute-start(bf16[128,2048]{1,0:T(8,128)(2,1)} %bitcast.46), channel_id=1, source_target_pairs={{0,16},{8,24},{16,0},{24,8},{1,17},{9,25},{17,1},{25,9},{2,18},{10... | collective-permute-start | bytes 1572872 | tf_op jit(solution)/shard_map/ppermute | solution.py:60
  85.7 9.4 %collective-permute-start.37 = (f32[2048]{0:T(1024)S(1)}, f32[2048]{0:T(1024)S(1)}, u32[]{:S(2)}, u32[]{:S(2)}) collective-permute-start(f32[2048]{0:T(1024)S(1)} %convert_reduce_fusion), channel_id=1, source_target_pairs={{0,1},{1,0},{2,3},{3,2},{4,5},{5,4},{6,7},{7,6},{8,9},{9,8},{10,11... | collective-permute-start | bytes 24584 | tf_op jit(solution)/shard_map/ppermute | solution.py:66
  86.1 9.0 %collective-permute-start.38 = (f32[2048]{0:T(1024)S(1)}, f32[2048]{0:T(1024)S(1)}, u32[]{:S(2)}, u32[]{:S(2)}) collective-permute-start(f32[2048]{0:T(1024)S(1)} %convert_reduce_fusion), channel_id=1, source_target_pairs={{0,2},{1,3},{2,0},{3,1},{4,6},{5,7},{6,4},{7,5},{8,10},{9,11},{10,... | collective-permute-start | bytes 24584 | tf_op jit(solution)/shard_map/ppermute | solution.py:66
  102.8 15.8 %collective-permute-start.7 = (bf16[128,2048]{1,0:T(8,128)(2,1)}, bf16[128,2048]{1,0:T(8,128)(2,1)}, u32[]{:S(2)}, u32[]{:S(2)}) collective-permute-start(bf16[128,2048]{1,0:T(8,128)(2,1)} %get-tuple-element.67), channel_id=1, source_target_pairs={{0,8},{8,0},{16,24},{24,16},{1,9},{9,1},{17,25},{25,17},{2,10},{10... | collective-permute-start | bytes 1572872 | tf_op jit(solution)/shard_map/ppermute | solution.py:60
  104.3 36.0 %collective-permute-start.8 = (bf16[128,2048]{1,0:T(8,128)(2,1)}, bf16[128,2048]{1,0:T(8,128)(2,1)}, u32[]{:S(2)}, u32[]{:S(2)}) collective-permute-start(bf16[128,2048]{1,0:T(8,128)(2,1)} %get-tuple-element.67), channel_id=1, source_target_pairs={{0,16},{8,24},{16,0},{24,8},{1,17},{9,25},{17,1},{25,9},{2,18},{10... | collective-permute-start | bytes 1572872 | tf_op jit(solution)/shard_map/ppermute | solution.py:60
  106.5 35.7 %collective-permute-start.9 = (bf16[128,2048]{1,0:T(8,128)(2,1)}, bf16[128,2048]{1,0:T(8,128)(2,1)}, u32[]{:S(2)}, u32[]{:S(2)}) collective-permute-start(bf16[128,2048]{1,0:T(8,128)(2,1)} %get-tuple-element.67), channel_id=1, source_target_pairs={{0,24},{8,16},{16,8},{24,0},{1,25},{9,17},{17,9},{25,1},{2,26},{10... | collective-permute-start | bytes 1572872 | tf_op jit(solution)/shard_map/ppermute | solution.py:60
  108.3 10.4 %all-to-all-start.4 = ((f32[8,4,256]{2,1,0:T(4,128)}), f32[8,4,256]{2,1,0:T(4,128)S(1)}, u32[]{:S(2)}, u32[]{:S(2)}) async-start(f32[8,4,256]{2,1,0:T(4,128)} %bitcast.594), calls=%async_computation.4 | async-start | bytes 65536 | tf_op jit(solution)/shard_map/all_to_all | solution.py:204
  118.7 29.3 %collective-permute-start.15 = (bf16[128,2048]{1,0:T(8,128)(2,1)}, bf16[128,2048]{1,0:T(8,128)(2,1)S(1)}, u32[]{:S(2)}, u32[]{:S(2)}) collective-permute-start(bf16[128,2048]{1,0:T(8,128)(2,1)} %bitcast.46), channel_id=1, source_target_pairs={{0,24},{8,16},{16,8},{24,0},{1,25},{9,17},{17,9},{25,1},{2,26},{10... | collective-permute-start | bytes 1572872 | tf_op jit(solution)/shard_map/ppermute | solution.py:60
  188.7 16.1 %collective-permute-start.66 = (bf16[1,512]{1,0:T(2,128)(2,1)S(1)}, bf16[1,512]{1,0:T(2,128)(2,1)S(1)}, u32[]{:S(2)}, u32[]{:S(2)}) collective-permute-start(bf16[1,512]{1,0:T(2,128)(2,1)S(1)} %get-tuple-element.63), channel_id=1, source_target_pairs={{0,8},{8,0},{16,24},{24,16},{1,9},{9,1},{17,25},{25,17},{2,10},{10... | collective-permute-start | bytes 3080 | tf_op jit(solution)/shard_map/ppermute | solution.py:60
  190.2 15.2 %collective-permute-start.67 = (bf16[1,512]{1,0:T(2,128)(2,1)S(1)}, bf16[1,512]{1,0:T(2,128)(2,1)S(1)}, u32[]{:S(2)}, u32[]{:S(2)}) collective-permute-start(bf16[1,512]{1,0:T(2,128)(2,1)S(1)} %get-tuple-element.63), channel_id=1, source_target_pairs={{0,16},{8,24},{16,0},{24,8},{1,17},{9,25},{17,1},{25,9},{2,18},{10... | collective-permute-start | bytes 3080 | tf_op jit(solution)/shard_map/ppermute | solution.py:60
  191.7 13.8 %collective-permute-start.68 = (bf16[1,512]{1,0:T(2,128)(2,1)S(1)}, bf16[1,512]{1,0:T(2,128)(2,1)S(1)}, u32[]{:S(2)}, u32[]{:S(2)}) collective-permute-start(bf16[1,512]{1,0:T(2,128)(2,1)S(1)} %get-tuple-element.63), channel_id=1, source_target_pairs={{0,24},{8,16},{16,8},{24,0},{1,25},{9,17},{17,9},{25,1},{2,26},{10... | collective-permute-start | bytes 3080 | tf_op jit(solution)/shard_map/ppermute | solution.py:60
  199.5 16.5 %collective-permute-start.10 = (bf16[144,2048]{1,0:T(8,128)(2,1)}, bf16[144,2048]{1,0:T(8,128)(2,1)}, u32[]{:S(2)}, u32[]{:S(2)}) collective-permute-start(bf16[144,2048]{1,0:T(8,128)(2,1)} %get-tuple-element.45), channel_id=1, source_target_pairs={{0,8},{8,0},{16,24},{24,16},{1,9},{9,1},{17,25},{25,17},{2,10},{10... | collective-permute-start | bytes 1769480 | tf_op jit(solution)/shard_map/ppermute | solution.py:60
  201.0 28.1 %collective-permute-start.11 = (bf16[144,2048]{1,0:T(8,128)(2,1)}, bf16[144,2048]{1,0:T(8,128)(2,1)}, u32[]{:S(2)}, u32[]{:S(2)}) collective-permute-start(bf16[144,2048]{1,0:T(8,128)(2,1)} %get-tuple-element.47), channel_id=1, source_target_pairs={{0,16},{8,24},{16,0},{24,8},{1,17},{9,25},{17,1},{25,9},{2,18},{10... | collective-permute-start | bytes 1769480 | tf_op jit(solution)/shard_map/ppermute | solution.py:60
  204.8 24.3 %collective-permute-start.12 = (bf16[144,2048]{1,0:T(8,128)(2,1)}, bf16[144,2048]{1,0:T(8,128)(2,1)S(1)}, u32[]{:S(2)}, u32[]{:S(2)}) collective-permute-start(bf16[144,2048]{1,0:T(8,128)(2,1)} %get-tuple-element.46), channel_id=1, source_target_pairs={{0,24},{8,16},{16,8},{24,0},{1,25},{9,17},{17,9},{25,1},{2,26},{10... | collective-permute-start | bytes 1769480 | tf_op jit(solution)/shard_map/ppermute | solution.py:60
  231.7 31.9 %collective-permute-start.16 = (bf16[144,2048]{1,0:T(8,128)(2,1)S(1)}, bf16[144,2048]{1,0:T(8,128)(2,1)S(1)}, u32[]{:S(2)}, u32[]{:S(2)}) collective-permute-start(bf16[144,2048]{1,0:T(8,128)(2,1)S(1)} %multiply_convert_fusion.1), channel_id=1, source_target_pairs={{0,8},{8,0},{16,24},{24,16},{1,9},{9,1},{17,25},{25,17},{2,10},{10... | collective-permute-start | bytes 1769480 | tf_op jit(solution)/shard_map/ppermute | solution.py:60
  232.8 30.8 %collective-permute-start.17 = (bf16[144,2048]{1,0:T(8,128)(2,1)S(1)}, bf16[144,2048]{1,0:T(8,128)(2,1)S(1)}, u32[]{:S(2)}, u32[]{:S(2)}) collective-permute-start(bf16[144,2048]{1,0:T(8,128)(2,1)S(1)} %multiply_convert_fusion.1), channel_id=1, source_target_pairs={{0,16},{8,24},{16,0},{24,8},{1,17},{9,25},{17,1},{25,9},{2,18},{10... | collective-permute-start | bytes 1769480 | tf_op jit(solution)/shard_map/ppermute | solution.py:60
  233.8 29.9 %collective-permute-start.18 = (bf16[144,2048]{1,0:T(8,128)(2,1)S(1)}, bf16[144,2048]{1,0:T(8,128)(2,1)S(1)}, u32[]{:S(2)}, u32[]{:S(2)}) collective-permute-start(bf16[144,2048]{1,0:T(8,128)(2,1)S(1)} %multiply_convert_fusion.1), channel_id=1, source_target_pairs={{0,24},{8,16},{16,8},{24,0},{1,25},{9,17},{17,9},{25,1},{2,26},{10... | collective-permute-start | bytes 1769480 | tf_op jit(solution)/shard_map/ppermute | solution.py:60
  235.3 23.6 %collective-permute-start.47 = (f32[2048]{0:T(1024)S(1)}, f32[2048]{0:T(1024)S(1)}, u32[]{:S(2)}, u32[]{:S(2)}) collective-permute-start(f32[2048]{0:T(1024)S(1)} %bitcast.758), channel_id=1, source_target_pairs={{0,8},{8,0},{16,24},{24,16},{1,9},{9,1},{17,25},{25,17},{2,10},{10... | collective-permute-start | bytes 24584 | tf_op jit(solution)/shard_map/ppermute | solution.py:60
  236.5 25.1 %collective-permute-start.48 = (f32[2048]{0:T(1024)S(1)}, f32[2048]{0:T(1024)S(1)}, u32[]{:S(2)}, u32[]{:S(2)}) collective-permute-start(f32[2048]{0:T(1024)S(1)} %bitcast.759), channel_id=1, source_target_pairs={{0,16},{8,24},{16,0},{24,8},{1,17},{9,25},{17,1},{25,9},{2,18},{10... | collective-permute-start | bytes 24584 | tf_op jit(solution)/shard_map/ppermute | solution.py:60
  280.5 16.6 %collective-permute-start.22 = (bf16[144,2048]{1,0:T(8,128)(2,1)}, bf16[144,2048]{1,0:T(8,128)(2,1)}, u32[]{:S(2)}, u32[]{:S(2)}) collective-permute-start(bf16[144,2048]{1,0:T(8,128)(2,1)} %get-tuple-element.42), channel_id=1, source_target_pairs={{0,8},{8,0},{16,24},{24,16},{1,9},{9,1},{17,25},{25,17},{2,10},{10... | collective-permute-start | bytes 1769480 | tf_op jit(solution)/shard_map/ppermute | solution.py:60
  281.9 25.7 %collective-permute-start.23 = (bf16[144,2048]{1,0:T(8,128)(2,1)}, bf16[144,2048]{1,0:T(8,128)(2,1)}, u32[]{:S(2)}, u32[]{:S(2)}) collective-permute-start(bf16[144,2048]{1,0:T(8,128)(2,1)} %get-tuple-element.44), channel_id=1, source_target_pairs={{0,16},{8,24},{16,0},{24,8},{1,17},{9,25},{17,1},{25,9},{2,18},{10... | collective-permute-start | bytes 1769480 | tf_op jit(solution)/shard_map/ppermute | solution.py:60
  282.5 25.1 %collective-permute-start.24 = (bf16[144,2048]{1,0:T(8,128)(2,1)}, bf16[144,2048]{1,0:T(8,128)(2,1)}, u32[]{:S(2)}, u32[]{:S(2)}) collective-permute-start(bf16[144,2048]{1,0:T(8,128)(2,1)} %get-tuple-element.43), channel_id=1, source_target_pairs={{0,24},{8,16},{16,8},{24,0},{1,25},{9,17},{17,9},{25,1},{2,26},{10... | collective-permute-start | bytes 1769480 | tf_op jit(solution)/shard_map/ppermute | solution.py:60
  310.6 12.0 %collective-permute-start.35 = (f32[2048]{0:T(1024)S(1)}, f32[2048]{0:T(1024)S(1)}, u32[]{:S(2)}, u32[]{:S(2)}) collective-permute-start(f32[2048]{0:T(1024)S(1)} %bitcast.762), channel_id=1, source_target_pairs={{0,16},{8,24},{16,0},{24,8},{1,17},{9,25},{17,1},{25,9},{2,18},{10... | collective-permute-start | bytes 24584 | tf_op jit(solution)/shard_map/ppermute | solution.py:60
  312.1 10.8 %collective-permute-start.36 = (f32[2048]{0:T(1024)S(1)}, f32[2048]{0:T(1024)S(1)}, u32[]{:S(2)}, u32[]{:S(2)}) collective-permute-start(f32[2048]{0:T(1024)S(1)} %bitcast.763), channel_id=1, source_target_pairs={{0,24},{8,16},{16,8},{24,0},{1,25},{9,17},{17,9},{25,1},{2,26},{10... | collective-permute-start | bytes 24584 | tf_op jit(solution)/shard_map/ppermute | solution.py:60
  314.3 22.5 %collective-permute-start.25 = (bf16[144,2048]{1,0:T(8,128)(2,1)S(1)}, bf16[144,2048]{1,0:T(8,128)(2,1)}, u32[]{:S(2)}, u32[]{:S(2)}) collective-permute-start(bf16[144,2048]{1,0:T(8,128)(2,1)S(1)} %multiply_convert_fusion), channel_id=1, source_target_pairs={{0,8},{8,0},{16,24},{24,16},{1,9},{9,1},{17,25},{25,17},{2,10},{10... | collective-permute-start | bytes 1769480 | tf_op jit(solution)/shard_map/ppermute | solution.py:60
  314.6 23.8 %collective-permute-start.26 = (bf16[144,2048]{1,0:T(8,128)(2,1)S(1)}, bf16[144,2048]{1,0:T(8,128)(2,1)}, u32[]{:S(2)}, u32[]{:S(2)}) collective-permute-start(bf16[144,2048]{1,0:T(8,128)(2,1)S(1)} %multiply_convert_fusion), channel_id=1, source_target_pairs={{0,16},{8,24},{16,0},{24,8},{1,17},{9,25},{17,1},{25,9},{2,18},{10... | collective-permute-start | bytes 1769480 | tf_op jit(solution)/shard_map/ppermute | solution.py:60
  316.2 22.3 %collective-permute-start.27 = (bf16[144,2048]{1,0:T(8,128)(2,1)S(1)}, bf16[144,2048]{1,0:T(8,128)(2,1)}, u32[]{:S(2)}, u32[]{:S(2)}) collective-permute-start(bf16[144,2048]{1,0:T(8,128)(2,1)S(1)} %multiply_convert_fusion), channel_id=1, source_target_pairs={{0,24},{8,16},{16,8},{24,0},{1,25},{9,17},{17,9},{25,1},{2,26},{10... | collective-permute-start | bytes 1769480 | tf_op jit(solution)/shard_map/ppermute | solution.py:60
  322.6 79.5 %collective-permute-start.31 = (f32[1,2048]{1,0:T(1,128)S(1)}, f32[1,2048]{1,0:T(1,128)S(1)}, u32[]{:S(2)}, u32[]{:S(2)}) collective-permute-start(f32[1,2048]{1,0:T(1,128)S(1)} %bitcast.717), channel_id=1, source_target_pairs={{0,8},{8,0},{16,24},{24,16},{1,9},{9,1},{17,25},{25,17},{2,10},{10... | collective-permute-start | bytes 24584 | tf_op jit(solution)/shard_map/ppermute | solution.py:60
  322.9 81.7 %collective-permute-start.32 = (f32[1,2048]{1,0:T(1,128)S(1)}, f32[1,2048]{1,0:T(1,128)S(1)}, u32[]{:S(2)}, u32[]{:S(2)}) collective-permute-start(f32[1,2048]{1,0:T(1,128)S(1)} %bitcast.718), channel_id=1, source_target_pairs={{0,16},{8,24},{16,0},{24,8},{1,17},{9,25},{17,1},{25,9},{2,18},{10... | collective-permute-start | bytes 24584 | tf_op jit(solution)/shard_map/ppermute | solution.py:60
  336.8 68.3 %collective-permute-start.33 = (f32[1,2048]{1,0:T(1,128)S(1)}, f32[1,2048]{1,0:T(1,128)S(1)}, u32[]{:S(2)}, u32[]{:S(2)}) collective-permute-start(f32[1,2048]{1,0:T(1,128)S(1)} %bitcast.719), channel_id=1, source_target_pairs={{0,24},{8,16},{16,8},{24,0},{1,25},{9,17},{17,9},{25,1},{2,26},{10... | collective-permute-start | bytes 24584 | tf_op jit(solution)/shard_map/ppermute | solution.py:60
  349.5 56.8 %collective-permute-start.44 = (f32[4,2048]{1,0:T(4,128)S(1)}, f32[4,2048]{1,0:T(4,128)S(1)}, u32[]{:S(2)}, u32[]{:S(2)}) collective-permute-start(f32[4,2048]{1,0:T(4,128)S(1)} %fusion.333), channel_id=1, source_target_pairs={{0,8},{8,0},{16,24},{24,16},{1,9},{9,1},{17,25},{25,17},{2,10},{10... | collective-permute-start | bytes 98312 | tf_op jit(solution)/shard_map/ppermute | solution.py:60
  350.9 55.4 %collective-permute-start.45 = (f32[4,2048]{1,0:T(4,128)S(1)}, f32[4,2048]{1,0:T(4,128)S(1)}, u32[]{:S(2)}, u32[]{:S(2)}) collective-permute-start(f32[4,2048]{1,0:T(4,128)S(1)} %fusion.333), channel_id=1, source_target_pairs={{0,16},{8,24},{16,0},{24,8},{1,17},{9,25},{17,1},{25,9},{2,18},{10... | collective-permute-start | bytes 98312 | tf_op jit(solution)/shard_map/ppermute | solution.py:60
  404.6 133.4 %collective-permute-start.28 = (bf16[144,2048]{1,0:T(8,128)(2,1)}, bf16[144,2048]{1,0:T(8,128)(2,1)}, u32[]{:S(2)}, u32[]{:S(2)}) collective-permute-start(bf16[144,2048]{1,0:T(8,128)(2,1)} %get-tuple-element.39), channel_id=1, source_target_pairs={{0,8},{8,0},{16,24},{24,16},{1,9},{9,1},{17,25},{25,17},{2,10},{10... | collective-permute-start | bytes 1769480 | tf_op jit(solution)/shard_map/ppermute | solution.py:60
  405.1 132.8 %collective-permute-start.29 = (bf16[144,2048]{1,0:T(8,128)(2,1)}, bf16[144,2048]{1,0:T(8,128)(2,1)}, u32[]{:S(2)}, u32[]{:S(2)}) collective-permute-start(bf16[144,2048]{1,0:T(8,128)(2,1)} %get-tuple-element.41), channel_id=1, source_target_pairs={{0,16},{8,24},{16,0},{24,8},{1,17},{9,25},{17,1},{25,9},{2,18},{10... | collective-permute-start | bytes 1769480 | tf_op jit(solution)/shard_map/ppermute | solution.py:60
  412.7 8.4 %collective-permute-start.50 = (f32[4,2048]{1,0:T(4,128)S(1)}, f32[4,2048]{1,0:T(4,128)S(1)}, u32[]{:S(2)}, u32[]{:S(2)}) collective-permute-start(f32[4,2048]{1,0:T(4,128)S(1)} %fusion.229), channel_id=1, source_target_pairs={{0,8},{8,0},{16,24},{24,16},{1,9},{9,1},{17,25},{25,17},{2,10},{10... | collective-permute-start | bytes 98312 | tf_op jit(solution)/shard_map/ppermute | solution.py:60
  414.6 7.1 %collective-permute-start.51 = (f32[4,2048]{1,0:T(4,128)S(1)}, f32[4,2048]{1,0:T(4,128)S(1)}, u32[]{:S(2)}, u32[]{:S(2)}) collective-permute-start(f32[4,2048]{1,0:T(4,128)S(1)} %fusion.229), channel_id=1, source_target_pairs={{0,16},{8,24},{16,0},{24,8},{1,17},{9,25},{17,1},{25,9},{2,18},{10... | collective-permute-start | bytes 98312 | tf_op jit(solution)/shard_map/ppermute | solution.py:60
  438.0 6.8 %collective-permute-start.56 = (bf16[8,2176]{1,0:T(8,128)(2,1)S(1)}, bf16[8,2176]{1,0:T(8,128)(2,1)S(1)}, u32[]{:S(2)}, u32[]{:S(2)}) collective-permute-start(bf16[8,2176]{1,0:T(8,128)(2,1)S(1)} %squeeze.129), channel_id=1, source_target_pairs={{0,8},{8,0},{16,24},{24,16},{1,9},{9,1},{17,25},{25,17},{2,10},{10... | collective-permute-start | bytes 104456 | tf_op jit(solution)/shard_map/ppermute | solution.py:60
  444.8 10.8 %collective-permute-start.59 = (bf16[4,4608]{1,0:T(4,128)(2,1)S(1)}, bf16[4,4608]{1,0:T(4,128)(2,1)}, u32[]{:S(2)}, u32[]{:S(2)}) collective-permute-start(bf16[4,4608]{1,0:T(4,128)(2,1)S(1)} %constant_dynamic-update-slice_fusion.10), channel_id=1, source_target_pairs={{0,1},{1,0},{2,3},{3,2},{4,5},{5,4},{6,7},{7,6},{8,9},{9,8},{10,11... | collective-permute-start | bytes 110600 | tf_op jit(solution)/shard_map/ppermute | solution.py:66
  444.9 13.8 %collective-permute-start.60 = (bf16[4,4608]{1,0:T(4,128)(2,1)S(1)}, bf16[4,4608]{1,0:T(4,128)(2,1)}, u32[]{:S(2)}, u32[]{:S(2)}) collective-permute-start(bf16[4,4608]{1,0:T(4,128)(2,1)S(1)} %constant_dynamic-update-slice_fusion.10), channel_id=1, source_target_pairs={{0,2},{1,3},{2,0},{3,1},{4,6},{5,7},{6,4},{7,5},{8,10},{9,11},{10,... | collective-permute-start | bytes 110600 | tf_op jit(solution)/shard_map/ppermute | solution.py:66
  446.2 15.3 %collective-permute-start.61 = (bf16[4,4608]{1,0:T(4,128)(2,1)S(1)}, bf16[4,4608]{1,0:T(4,128)(2,1)}, u32[]{:S(2)}, u32[]{:S(2)}) collective-permute-start(bf16[4,4608]{1,0:T(4,128)(2,1)S(1)} %constant_dynamic-update-slice_fusion.10), channel_id=1, source_target_pairs={{0,3},{1,2},{2,1},{3,0},{4,7},{5,6},{6,5},{7,4},{8,11},{9,10},{10,... | collective-permute-start | bytes 110600 | tf_op jit(solution)/shard_map/ppermute | solution.py:66
  451.9 35.2 %all-to-all-start.6 = ((bf16[32,2,1088]{2,1,0:T(2,128)(2,1)}), bf16[32,2,1088]{2,1,0:T(2,128)(2,1)S(1)}, u32[]{:S(2)}, u32[]{:S(2)}) async-start(bf16[32,2,1088]{2,1,0:T(2,128)(2,1)} %reshape.1403), calls=%async_computation.6 | async-start | bytes 294912 | tf_op jit(solution)/shard_map/all_to_all | solution.py:295
  455.6 9.3 %collective-permute-start.53 = (bf16[9,2192]{1,0:T(8,128)(2,1)}, bf16[9,2192]{1,0:T(8,128)(2,1)S(1)}, u32[]{:S(2)}, u32[]{:S(2)}) collective-permute-start(bf16[9,2192]{1,0:T(8,128)(2,1)} %get-tuple-element.82), channel_id=1, source_target_pairs={{0,8},{8,0},{16,24},{24,16},{1,9},{9,1},{17,25},{25,17},{2,10},{10... | collective-permute-start | bytes 118376 | tf_op jit(solution)/shard_map/ppermute | solution.py:60
  458.6 7.9 %collective-permute-start.54 = (bf16[9,2192]{1,0:T(8,128)(2,1)}, bf16[9,2192]{1,0:T(8,128)(2,1)S(1)}, u32[]{:S(2)}, u32[]{:S(2)}) collective-permute-start(bf16[9,2192]{1,0:T(8,128)(2,1)} %get-tuple-element.81), channel_id=1, source_target_pairs={{0,16},{8,24},{16,0},{24,8},{1,17},{9,25},{17,1},{25,9},{2,18},{10... | collective-permute-start | bytes 118376 | tf_op jit(solution)/shard_map/ppermute | solution.py:60
  461.5 7.5 %collective-permute-start.55 = (bf16[9,2192]{1,0:T(8,128)(2,1)}, bf16[9,2192]{1,0:T(8,128)(2,1)S(1)}, u32[]{:S(2)}, u32[]{:S(2)}) collective-permute-start(bf16[9,2192]{1,0:T(8,128)(2,1)} %get-tuple-element.80), channel_id=1, source_target_pairs={{0,24},{8,16},{16,8},{24,0},{1,25},{9,17},{17,9},{25,1},{2,26},{10... | collective-permute-start | bytes 118376 | tf_op jit(solution)/shard_map/ppermute | solution.py:60
  464.9 11.3 %collective-permute-start.69 = (bf16[4,9216]{1,0:T(4,128)(2,1)}, bf16[4,9216]{1,0:T(4,128)(2,1)S(1)}, u32[]{:S(2)}, u32[]{:S(2)}) collective-permute-start(bf16[4,9216]{1,0:T(4,128)(2,1)} %get-tuple-element.25), channel_id=1, source_target_pairs={{0,1},{1,0},{2,3},{3,2},{4,5},{5,4},{6,7},{7,6},{8,9},{9,8},{10,11... | collective-permute-start | bytes 221192 | tf_op jit(solution)/shard_map/ppermute | solution.py:66
  466.6 11.0 %collective-permute-start.70 = (bf16[4,9216]{1,0:T(4,128)(2,1)}, bf16[4,9216]{1,0:T(4,128)(2,1)}, u32[]{:S(2)}, u32[]{:S(2)}) collective-permute-start(bf16[4,9216]{1,0:T(4,128)(2,1)} %get-tuple-element.25), channel_id=1, source_target_pairs={{0,2},{1,3},{2,0},{3,1},{4,6},{5,7},{6,4},{7,5},{8,10},{9,11},{10,... | collective-permute-start | bytes 221192 | tf_op jit(solution)/shard_map/ppermute | solution.py:66
  469.1 8.5 %collective-permute-start.71 = (bf16[4,9216]{1,0:T(4,128)(2,1)}, bf16[4,9216]{1,0:T(4,128)(2,1)}, u32[]{:S(2)}, u32[]{:S(2)}) collective-permute-start(bf16[4,9216]{1,0:T(4,128)(2,1)} %get-tuple-element.25), channel_id=1, source_target_pairs={{0,3},{1,2},{2,1},{3,0},{4,7},{5,6},{6,5},{7,4},{8,11},{9,10},{10,... | collective-permute-start | bytes 221192 | tf_op jit(solution)/shard_map/ppermute | solution.py:66
  476.2 61.8 %collective-permute-start.30 = (bf16[144,2048]{1,0:T(8,128)(2,1)}, bf16[144,2048]{1,0:T(8,128)(2,1)}, u32[]{:S(2)}, u32[]{:S(2)}) collective-permute-start(bf16[144,2048]{1,0:T(8,128)(2,1)} %get-tuple-element.40), channel_id=1, source_target_pairs={{0,24},{8,16},{16,8},{24,0},{1,25},{9,17},{17,9},{25,1},{2,26},{10... | collective-permute-start | bytes 1769480 | tf_op jit(solution)/shard_map/ppermute | solution.py:60
  479.5 27.2 %collective-permute-start.72 = (bf16[4,4,9216]{2,1,0:T(4,128)(2,1)}, bf16[4,4,9216]{2,1,0:T(4,128)(2,1)}, u32[]{:S(2)}, u32[]{:S(2)}) collective-permute-start(bf16[4,4,9216]{2,1,0:T(4,128)(2,1)} %pad_maximum_fusion.10), channel_id=1, source_target_pairs={{0,4},{4,0},{1,5},{5,1},{2,6},{6,2},{3,7},{7,3},{8,12},{12,8},{9,1... | collective-permute-start | bytes 884744 | tf_op jit(solution)/shard_map/ppermute | solution.py:63
  484.5 30.1 %collective-permute-start.65 = (bf16[8,4,4608]{2,1,0:T(4,128)(2,1)}, bf16[8,4,4608]{2,1,0:T(4,128)(2,1)}, u32[]{:S(2)}, u32[]{:S(2)}) collective-permute-start(bf16[8,4,4608]{2,1,0:T(4,128)(2,1)} %constant_dynamic-update-slice_fusion.16), channel_id=1, source_target_pairs={{0,24},{8,16},{16,8},{24,0},{1,25},{9,17},{17,9},{25,1},{2,26},{10... | collective-permute-start | bytes 884744 | tf_op jit(solution)/shard_map/ppermute | solution.py:60
  487.1 13.4 %all-to-all-start.5 = ((bf16[32,2,1152]{2,1,0:T(2,128)(2,1)}), bf16[32,2,1152]{2,1,0:T(2,128)(2,1)}, u32[]{:S(2)}, u32[]{:S(2)}) async-start(bf16[32,2,1152]{2,1,0:T(2,128)(2,1)} %reshape.1401), calls=%async_computation.5 | async-start | bytes 294912 | tf_op jit(solution)/shard_map/all_to_all | solution.py:339
  506.7 11.3 %collective-permute-start.64 = (bf16[8,4,4608]{2,1,0:T(4,128)(2,1)}, bf16[8,4,4608]{2,1,0:T(4,128)(2,1)}, u32[]{:S(2)}, u32[]{:S(2)}) collective-permute-start(bf16[8,4,4608]{2,1,0:T(4,128)(2,1)} %constant_dynamic-update-slice_fusion.16), channel_id=1, source_target_pairs={{0,16},{8,24},{16,0},{24,8},{1,17},{9,25},{17,1},{25,9},{2,18},{10... | collective-permute-start | bytes 884744 | tf_op jit(solution)/shard_map/ppermute | solution.py:60
  514.6 8.5 %collective-permute-start.63 = (bf16[8,4,4608]{2,1,0:T(4,128)(2,1)}, bf16[8,4,4608]{2,1,0:T(4,128)(2,1)S(1)}, u32[]{:S(2)}, u32[]{:S(2)}) collective-permute-start(bf16[8,4,4608]{2,1,0:T(4,128)(2,1)} %constant_dynamic-update-slice_fusion.16), channel_id=1, source_target_pairs={{0,8},{8,0},{16,24},{24,16},{1,9},{9,1},{17,25},{25,17},{2,10},{10... | collective-permute-start | bytes 884744 | tf_op jit(solution)/shard_map/ppermute | solution.py:60
  (90 other events, 724.8 us)
Sparse Core Ops, SparseCore 0:
  20.3 28.8 all-gather.13
  50.8 47.3 all-gather.11
  99.8 64.0 all-gather.7
  165.4 27.6 all-gather.9
  194.5 28.5 all-gather.15
  225.2 81.5 all-gather.17
  308.4 80.5 all-gather.19
